TPU v7x, 32 devices: a whole 2x2x4 slice. The times are simulated.
32 devices in a mesh: dp: 16 (over z, y, x), pair: 2 (over core).
Axes of the slice: x: 2, y: 2, z: 4, core: 2. Of those that a mesh axis runs over, the one named last changes fastest.
Arguments:
- latents: bfloat16 [2, 64, 256, 384], P(None, ('dp', 'pair')), may hold values from -6 to 6
- conditions: bfloat16 [2, 64, 384], P(None, ('dp', 'pair')), may hold values from -6 to 6
- counts: int32 [2, 32], P(None, ('dp', 'pair')), may hold values from 1 to 2, as said below
- cotangent: bfloat16 [2, 64, 256, 384], P(None, ('dp', 'pair')), may hold values from -6 to 6
- w_ada: float32 [384, 2304], P('dp', 'pair'), may hold values from -0.3125 to 0.3125
- w_qkv: float32 [384, 1152], P('dp', 'pair'), may hold values from -0.3125 to 0.3125
- w_proj: float32 [384, 384], P('dp', 'pair'), may hold values from -0.4375 to 0.4375
- w_fc1: float32 [384, 1536], P('dp', 'pair'), may hold values from -0.3125 to 0.3125
- w_fc2: float32 [1536, 384], P('pair', 'dp'), may hold values from -0.15625 to 0.15625
- biases: float32 [5376], P(('dp', 'pair')), may hold values from -3 to 3
- m_ada: float32 [384, 2304], P('dp', 'pair')
- m_qkv: float32 [384, 1152], P('dp', 'pair')
- m_proj: float32 [384, 384], P('dp', 'pair')
- m_fc1: float32 [384, 1536], P('dp', 'pair')
- m_fc2: float32 [1536, 384], P('pair', 'dp')
- bias_first: float32 [5376], P(('dp', 'pair'))
- bias_second: float32 [5376], P(('dp', 'pair')), as said below
Outputs:
- block_out: bfloat16 [2, 64, 256, 384], P(None, ('dp', 'pair'))
- grad_latents: float32 [2, 64, 256, 384], P(None, ('dp', 'pair'))
- grad_conditions: float32 [2, 64, 384], P(None, ('dp', 'pair'))
- new_m_ada: float32 [384, 2304], P('dp', 'pair')
- new_m_qkv: float32 [384, 1152], P('dp', 'pair')
- new_m_proj: float32 [384, 384], P('dp', 'pair')
- new_m_fc1: float32 [384, 1536], P('dp', 'pair')
- new_m_fc2: float32 [1536, 384], P('pair', 'dp')
- new_w_ada: float32 [384, 2304], P('dp', 'pair')
- new_w_qkv: float32 [384, 1152], P('dp', 'pair')
- new_w_proj: float32 [384, 384], P('dp', 'pair')
- new_w_fc1: float32 [384, 1536], P('dp', 'pair')
- new_w_fc2: float32 [1536, 384], P('pair', 'dp')
- bias_grad: float32 [5376], P(('dp', 'pair'))
- new_bias_second: float32 [5376], P(('dp', 'pair'))
- new_biases: float32 [5376], P(('dp', 'pair'))
Inputs may be any that keep to these rules, and one draw needn't show every extreme that they name: counts[b, g] live samples fill the first slots of device g in micro-batch b; the other slots are padding. `bias_second`: positive.
All inputs are finite; a program needn't handle non-finite values.
Results may differ from a plain program's by a relative error of at most 0.015.
The roundings to bfloat16 on the way count: a program that leaves them out, or rounds other values in their place, can miss the bound.
Values may be sent and summed in bfloat16 or wider, within the bound.
No kernel may reach another device: no remote copies, remote signals or barrier semaphores. Data moves between devices by JAX's collectives and lax.ppermute only.
A program may use at most 128 MiB of HBM per device.

v0:
```python
import functools
import math

import jax
import jax.numpy as jnp
from jax import lax
from jax.experimental import pallas as pl
from jax.experimental.pallas import tpu as pltpu
from jax.sharding import PartitionSpec as P

HD = 64
ITERS = 3
STEP = 10

coef_one = 3.4445
coef_two = -4.775
coef_three = 2.0315
momentum_decay = 0.95
matrix_rate = 0.5
bias_rate = 0.5
decay_rate = 0.01
first_decay = 0.9
second_decay = 0.95

AXES = ("dp", "pair")
F32 = jnp.float32
BF16 = jnp.bfloat16


def split_columns(value, extents):
    result = []
    offset = 0
    for extent in extents:
        result.append(value[..., offset : offset + extent])
        offset = offset + extent
    return result


def silu_plain(values):
    return values * jax.nn.sigmoid(values)


def dot(left, right):
    return jnp.dot(left, right, preferred_element_type=F32)


def dot_rows(left, right):
    return lax.dot_general(left, right, (((0,), (0,)), ((), ())), preferred_element_type=F32)


def dot_columns(left, right):
    return lax.dot_general(left, right, (((1,), (1,)), ((), ())), preferred_element_type=F32)


def struct(shape, kind):
    return jax.ShapeDtypeStruct(shape, kind)


def params():
    return pltpu.CompilerParams(
        dimension_semantics=("arbitrary",), vmem_limit_bytes=56 * 2**20
    )


def fused(body, *operands, plain=False):
    if plain:
        return body(*operands)
    results, tree = jax.tree.flatten(jax.eval_shape(body, *operands))
    count = len(operands)

    def kernel(*refs):
        values = body(*[ref[...] for ref in refs[:count]])
        for ref, value in zip(refs[count:], jax.tree.leaves(values)):
            ref[...] = value

    traffic = sum(member.size * 4 for member in list(operands) + results)
    outs = pl.pallas_call(
        kernel,
        out_shape=[struct(member.shape, member.dtype) for member in results],
        compiler_params=pltpu.CompilerParams(vmem_limit_bytes=56 * 2**20),
        cost_estimate=pl.CostEstimate(flops=0, bytes_accessed=traffic, transcendentals=0),
    )(*operands)
    return jax.tree.unflatten(tree, outs)


class Links:
    def __init__(self):
        self.groups = lax.axis_size("dp")
        self.me = lax.axis_index("dp")
        self.core = lax.axis_index("pair")
        self.quarter = self.groups // 4
        self.digits = []
        stride = 1
        while stride < self.quarter:
            radix = min(4, self.quarter // stride)
            self.digits.append((stride, radix))
            stride = stride * radix

    def swap(self, value, flips):
        pairs = []
        for group in range(self.groups):
            for core in range(2):
                pairs.append((2 * group + core, 2 * (group ^ flips[core]) + core))
        return lax.ppermute(value, AXES, pairs)

    def swap_pair(self, value):
        return lax.ppermute(value, AXES, [(i, i ^ 1) for i in range(2 * self.groups)])

    def far(self, value, stride, step):
        return self.swap(value, (4 * stride * step, 4 * stride * step))

    def gather_far(self, block, rows):
        held = block
        for stride, radix in self.digits:
            arrived = [self.far(held, stride, step) for step in range(1, radix)]

            def join(*pieces, rows=rows):
                wide = [piece.astype(F32) for piece in pieces]
                parts = [piece[:rows] for piece in wide]
                if rows < wide[0].shape[0]:
                    parts = parts + [piece[rows:] for piece in wide]
                return jnp.concatenate(parts, axis=0).astype(BF16)

            held = fused(join, held, *arrived, plain=rows % 8 > 0)
            rows = rows * radix
        return held

    def gather_near(self, held):
        second = self.swap(held, (2, 1))
        first = self.swap(held, (1, 2))
        return [held, second, first, self.swap(second, (1, 2))]

    def gather_direct(self, held):
        return [held] + [self.swap(held, flips) for flips in ((2, 1), (1, 2), (3, 3))]

    def swap_pairs(self, own):
        return [self.swap_pair(piece) for piece in own]

    def scatter(self, mine, give, direct):
        kept, arrived = mine, [self.swap_pair(give)]
        near = [lambda v, step: self.swap(v, (1, 2)), lambda v, step: self.swap(v, (2, 1))]
        plane = ((2, 1), (1, 2), (3, 3))
        if direct:
            phases = [(4, lambda v, step: self.swap(v, plane[step - 1]))]
        else:
            phases = [(2, send) for send in near]
        for stride, radix in reversed(self.digits):
            phases.append((radix, lambda v, step, stride=stride: self.far(v, stride, step)))
        for radix, send in phases:
            extent = kept.shape[0] // radix

            def add_split(kept, *arrived, radix=radix, extent=extent):
                for piece in arrived:
                    kept = kept + piece.astype(F32)
                return [kept[:extent]] + [
                    kept[step * extent : (step + 1) * extent].astype(BF16)
                    for step in range(1, radix)
                ]

            kept, *sent = fused(add_split, kept, *arrived, plain=extent % 8 > 0)
            arrived = [send(piece, step + 1) for step, piece in enumerate(sent)]
            yield kept, arrived

    def order(self, core, rows):
        extent = self.groups * rows
        row = lax.broadcasted_iota(jnp.int32, (extent, extent), 0)
        column = lax.broadcasted_iota(jnp.int32, (extent, extent), 1)
        relative = (row // rows) ^ self.me
        low, high = relative & 1, (relative >> 1) & 1
        first, second = (low, high) if core == 0 else (high, low)
        place = (first * 2 + second) * self.quarter + (relative >> 2)
        return (place * rows + row % rows == column).astype(BF16)

    def bias_places(self, core, rows, columns, shape, axis):
        row = lax.broadcasted_iota(jnp.int32, shape, axis)
        place = row // rows
        turn, distance = place // self.quarter, place % self.quarter
        first, second = turn // 2, turn % 2
        low, high = (first, second) if core == 0 else (second, first)
        group = (distance * 4 + high * 2 + low) ^ self.me
        return (2 * group + core) * rows * columns + row % rows * columns


def layer_stats(values):
    centred = values - jnp.mean(values, axis=-1, keepdims=True)
    spread = jnp.mean(centred * centred, axis=-1, keepdims=True)
    scale = lax.rsqrt(spread + 1e-06)
    return centred * scale, scale


def layer_back(normed, scale, grad):
    mean_grad = jnp.mean(grad, axis=-1, keepdims=True)
    mean_both = jnp.mean(grad * normed, axis=-1, keepdims=True)
    return scale * (grad - mean_grad - normed * mean_both)


def head_masks(rows):
    lane = lax.broadcasted_iota(jnp.int32, (rows, 2 * HD), 1)
    return lane < HD, lane >= HD


def column_sum(values):
    return jnp.sum(values, axis=0, keepdims=True)


def halves_of(core, own_refs, other_refs):
    own = jnp.concatenate([ref[...] for ref in own_refs], axis=0)
    other = jnp.concatenate([ref[...] for ref in other_refs], axis=0)
    return jnp.where(core == 0, own, other), jnp.where(core == 0, other, own)


def modes_kernel(place_ref, *refs):
    own_refs, other_refs = refs[:4], refs[4:8]
    cond_ref, orders_ref, lines_ref, lanes_ref = refs[8:12]
    wqkv_ref, bias_ref, modes_ref, act_ref = refs[12:]
    features = orders_ref.shape[0]
    ada_half = 3 * features
    qkv_half = 3 * features // 2
    halves = halves_of(place_ref[0], own_refs, other_refs)
    lines_extent = -(-bias_ref.shape[1] // 128 // 16) * 16
    lane = lax.broadcasted_iota(jnp.int32, (features, 128), 1)
    line = lax.broadcasted_iota(jnp.int32, (lines_extent, features), 0)
    lines = jnp.zeros((lines_extent, 128), F32)
    act = silu_plain(cond_ref[...].astype(F32)).astype(BF16)
    act_ref[...] = act
    raw_modes = []
    for side in range(2):
        order = orders_ref[:, side * features : (side + 1) * features]
        wqkv_ref[:, side * qkv_half : (side + 1) * qkv_half] = dot(
            order, halves[side][:, ada_half : ada_half + qkv_half]
        ).astype(BF16)
        raw_modes.append(dot(dot(act, order).astype(BF16), halves[side][:, :ada_half]))
        tail = halves[side][:, ada_half + qkv_half :].astype(F32)
        lanes_here = lanes_ref[:, side * 128 : (side + 1) * 128]
        lines_here = lines_ref[side : side + 1, :]
        for column in range(bias_ref.shape[1] // (2 * features)):
            spread = jnp.where(
                ((lanes_here + column) & 127) == lane, tail[:, column : column + 1], 0.0
            ).astype(BF16)
            chosen = jnp.where(((lines_here + column) >> 7) == line, 1.0, 0.0).astype(BF16)
            lines = lines + dot(chosen, spread)
    for index in range(bias_ref.shape[1] // 128):
        bias_ref[:, index * 128 : (index + 1) * 128] = lines[index : index + 1]
    modes = jnp.concatenate(raw_modes, axis=1) + bias_ref[:, : 6 * features]
    for index in range(modes_ref.shape[0]):
        modes_ref[index] = modes[index : index + 1]


def condition_kernel(place_ref, *refs):
    own_refs, other_refs = refs[:4], refs[4:8]
    grad_ref, cond_ref, orders_ref, out_ref = refs[8:]
    features = orders_ref.shape[0]
    half = 3 * features
    halves = halves_of(place_ref[0], own_refs, other_refs)
    grads = jnp.concatenate([grad_ref[index] for index in range(grad_ref.shape[0])], axis=0)
    total = jnp.zeros(cond_ref.shape, F32)
    for side in range(2):
        part = dot_columns(grads[:, side * half : (side + 1) * half], halves[side][:, :half])
        order = orders_ref[:, side * features : (side + 1) * features].astype(F32)
        total = total + lax.dot_general(
            part,
            order,
            (((1,), (1,)), ((), ())),
            precision=lax.Precision.HIGHEST,
            preferred_element_type=F32,
        )
    cond = cond_ref[...].astype(F32)
    gate = jax.nn.sigmoid(cond)
    out_ref[...] = total * (gate * (1.0 + cond * (1.0 - gate)))


def mix_kernel(x_ref, modes_ref, bias_ref, wqkv_ref, attn_in_ref, qkv_ref, lse_ref, mixed_ref):
    features = x_ref.shape[-1]
    length = x_ref.shape[-2]
    scale = HD ** (-0.5)
    masks = head_masks(length)
    offset = 6 * features
    normed, _ = layer_stats(x_ref[0].astype(F32))
    shifting, scaling = modes_ref[0, :, :features], modes_ref[0, :, features : 2 * features]
    attn_in = (normed * (1.0 + scaling) + shifting).astype(BF16)
    attn_in_ref[0] = attn_in
    query = dot(attn_in, wqkv_ref[:, :features]) + bias_ref[:, offset : offset + features]
    query = query.astype(BF16)
    key = dot(attn_in, wqkv_ref[:, features : 2 * features]).astype(BF16)
    value = dot(attn_in, wqkv_ref[:, 2 * features :])
    value = (value + bias_ref[:, offset + features : offset + 2 * features]).astype(BF16)
    qkv_ref[0, :, :features] = query
    qkv_ref[0, :, features : 2 * features] = key
    qkv_ref[0, :, 2 * features :] = value
    lane = lax.broadcasted_iota(jnp.int32, (length, 128), 1)
    log_totals = jnp.zeros((length, 128), F32)
    for block in range(features // (2 * HD)):
        window = slice(block * 2 * HD, (block + 1) * 2 * HD)
        pieces = []
        for side in range(2):
            key_side = jnp.where(masks[side], key[:, window], jnp.zeros((), BF16))
            scores = dot_columns(query[:, window], key_side) * scale
            row_max = jnp.max(scores, axis=-1, keepdims=True)
            terms = jnp.exp(scores - row_max)
            row_total = jnp.sum(terms, axis=-1, keepdims=True)
            probs = (terms / row_total).astype(BF16)
            pieces.append(dot(probs, value[:, window]))
            log_totals = jnp.where(
                lane == 2 * block + side, row_max + jnp.log(row_total), log_totals
            )
        mixed_ref[0, :, window] = jnp.where(masks[0], pieces[0], pieces[1]).astype(BF16)
    lse_ref[0] = log_totals


def hidden_kernel(place_ref, counts_ref, *refs):
    own_refs, other_refs = refs[:4], refs[4:8]
    x_ref, cot_ref, mixed_ref, modes_ref, bias_ref, order_ref = refs[8:14]
    out_ref, dmix_ref, dx_ref, dmodes_ref, dbias_ref, mine_ref, give_ref = refs[14:21]
    total_ref, fc1_ref, fc2_ref, wproj_ref = refs[21:]
    step = pl.program_id(0)
    core = place_ref[0]
    features = x_ref.shape[-1]
    length = x_ref.shape[-2]
    hidden = fc1_ref.shape[1]
    half = hidden // 2
    small = features // 2

    @pl.when(step == 0)
    def _():
        total_ref[...] = jnp.zeros_like(total_ref)
        dbias_ref[...] = jnp.zeros_like(dbias_ref)
        halves = halves_of(core, own_refs, other_refs)
        for side in range(2):
            order = order_ref[:, side * features : (side + 1) * features]
            sorted_half = dot(order, halves[side]).astype(BF16)
            fc1_ref[:, side * half : (side + 1) * half] = sorted_half[:, :half]
            fc2_ref[:, side * half : (side + 1) * half] = sorted_half[:, half:hidden]
            wproj_ref[:, side * small : (side + 1) * small] = sorted_half[
                :, hidden : hidden + small
            ]

    def mode(index):
        return modes_ref[0, :, index * features : (index + 1) * features]

    offset = 8 * features
    bias_proj = bias_ref[:, offset : offset + features]
    bias_fc1 = bias_ref[:, offset + features : offset + features + hidden]
    bias_fc2 = bias_ref[:, offset + features + hidden :]
    slots = pl.num_programs(0) // counts_ref.shape[0]
    live = (step % slots < counts_ref[step // slots, 0]).astype(F32)

    x = x_ref[0].astype(F32)
    mixed = mixed_ref[0]
    attn = dot(mixed, wproj_ref[...]) + bias_proj
    after = x + mode(2) * attn
    normed, spread = layer_stats(after)
    mlp_in = (normed * (1.0 + mode(4)) + mode(3)).astype(BF16)
    upstream = cot_ref[0].astype(F32) * live
    grad_mlp = (mode(5) * upstream).astype(BF16)
    mlp_in_ordered = dot(mlp_in, order_ref[...]).astype(BF16)
    grad_mlp_ordered = dot(grad_mlp, order_ref[...]).astype(BF16)
    mlp = jnp.zeros((length, features), F32)
    grad_mlp_in = jnp.zeros((length, features), F32)
    chunk = math.gcd(half, 256)
    for index in range(hidden // chunk):
        window = slice(index * chunk, (index + 1) * chunk)
        side = index * chunk // half
        inside = index * chunk - side * half
        sorted_rows = slice(side * features, (side + 1) * features)
        pre = dot(mlp_in, fc1_ref[:, window]) + bias_fc1[:, window]
        grad_act = dot(grad_mlp, fc2_ref[:, window])
        square = pre * pre
        inner = 0.7978845608028654 * (pre + 0.044715 * square * pre)
        bent = jnp.tanh(inner)
        risen = 0.5 * (1.0 + bent)
        act = (pre * risen).astype(BF16)
        slope = risen + 0.5 * pre * (1.0 - bent * bent) * (
            0.7978845608028654 * (1.0 + 3 * 0.044715 * square)
        )
        grad_pre = (grad_act * slope).astype(BF16)
        mlp = mlp + dot_columns(act, fc2_ref[:, window])
        grad_mlp_in = grad_mlp_in + dot_columns(grad_pre, fc1_ref[:, window])
        dbias_ref[:, features + index * chunk : features + (index + 1) * chunk] += column_sum(
            grad_pre.astype(F32)
        )
        total_ref[side, :, inside : inside + chunk] += dot_rows(
            mlp_in_ordered[:, sorted_rows], grad_pre
        )
        total_ref[side, :, half + inside : half + inside + chunk] += dot_rows(
            grad_mlp_ordered[:, sorted_rows], act
        )
    mlp = mlp + bias_fc2
    out_ref[0] = (after + mode(5) * mlp).astype(BF16)
    dmodes_ref[0, :, 5 * features :] = column_sum(upstream * mlp)
    dbias_ref[:, features + hidden :] += column_sum(grad_mlp.astype(F32))
    dmodes_ref[0, :, 4 * features : 5 * features] = column_sum(grad_mlp_in * normed)
    dmodes_ref[0, :, 3 * features : 4 * features] = column_sum(grad_mlp_in)
    grad_after = upstream + layer_back(normed, spread, grad_mlp_in * (1.0 + mode(4)))
    dx_ref[0] = grad_after
    dmodes_ref[0, :, 2 * features : 3 * features] = column_sum(grad_after * attn)
    dmodes_ref[0, :, : 2 * features] = jnp.zeros((1, 2 * features), F32)
    grad_attn = (mode(2) * grad_after).astype(BF16)
    dbias_ref[:, :features] += column_sum(grad_attn.astype(F32))
    dmix_ref[0] = dot_columns(grad_attn, wproj_ref[...]).astype(BF16)
    mixed_ordered = dot(mixed, order_ref[...]).astype(BF16)
    for side in range(2):
        total_ref[side, :, hidden : hidden + small] += dot_rows(
            mixed_ordered[:, side * features : (side + 1) * features],
            grad_attn[:, side * small : (side + 1) * small],
        )

    @pl.when(step == pl.num_programs(0) - 1)
    def _():
        mine_ref[...] = total_ref[core]
        give_ref[...] = total_ref[1 - core].astype(BF16)


def scores_kernel(qkv_ref, lse_ref, dmix_ref, grad_ref):
    features = dmix_ref.shape[-1]
    length = dmix_ref.shape[-2]
    scale = HD ** (-0.5)
    masks = head_masks(length)
    nothing = jnp.zeros((), BF16)
    for block in range(features // (2 * HD)):
        windows = [
            slice(member * features + block * 2 * HD, member * features + (block + 1) * 2 * HD)
            for member in range(3)
        ]
        query, key, value = [qkv_ref[0, :, window] for window in windows]
        dmix = dmix_ref[0, :, windows[0]]
        pieces = []
        for side in range(2):
            head = 2 * block + side
            scores = dot_columns(query, jnp.where(masks[side], key, nothing)) * scale
            probs = jnp.exp(scores - lse_ref[0, :, head : head + 1])
            grad_probs = dot_columns(jnp.where(masks[side], dmix, nothing), value)
            inner = jnp.sum(grad_probs * probs, axis=-1, keepdims=True)
            grad_scores = (probs * (grad_probs - inner)).astype(BF16)
            pieces.append(
                (
                    dot(grad_scores, key) * scale,
                    dot_rows(grad_scores, query) * scale,
                    dot_rows(probs.astype(BF16), dmix),
                )
            )
        for member in range(3):
            grad_ref[0, :, windows[member]] = jnp.where(
                masks[0], pieces[0][member], pieces[1][member]
            ).astype(BF16)


def closing_kernel(starts, place_ref, *refs):
    parts, refs = refs[: len(starts)], refs[len(starts) :]
    x_ref, dx_ref, modes_ref, attn_in_ref, first_ref, wqkv_ref, order_ref = refs[:7]
    grad_ref, dmodes_ref, dbias_ref, mine_ref, give_ref, total_ref = refs[7:]
    step = pl.program_id(0)
    features = x_ref.shape[-1]
    middle = features // 2

    @pl.when(step == 0)
    def _():
        total_ref[...] = jnp.zeros_like(total_ref)
        dbias_ref[...] = jnp.zeros_like(dbias_ref)

    grads = parts[0][0]
    for start, part in zip(starts[1:], parts[1:]):
        grads = jnp.where(step >= start, part[0], grads)
    dbias_ref[:, :features] += column_sum(grads[:, :features].astype(F32))
    dbias_ref[:, features:] += column_sum(grads[:, 2 * features :].astype(F32))
    ordered = dot(attn_in_ref[0], order_ref[...]).astype(BF16)
    for side in range(2):
        total_ref[side, :, : 3 * middle] += dot_rows(
            ordered[:, side * features : (side + 1) * features],
            grads[:, side * 3 * middle : (side + 1) * 3 * middle],
        )
    grad_attn_in = dot_columns(grads, wqkv_ref[...])
    normed, spread = layer_stats(x_ref[0].astype(F32))
    scaling = modes_ref[0, :, features : 2 * features]
    grad_ref[0] = dx_ref[0] + layer_back(normed, spread, grad_attn_in * (1.0 + scaling))
    dmodes_ref[0, :, :features] = column_sum(grad_attn_in).astype(BF16)
    dmodes_ref[0, :, features : 2 * features] = column_sum(grad_attn_in * normed).astype(BF16)
    dmodes_ref[0, :, 2 * features :] = first_ref[0, :, 2 * features :].astype(BF16)

    @pl.when(step == pl.num_programs(0) - 1)
    def _():
        core = place_ref[0]
        mine_ref[...] = total_ref[core]
        give_ref[...] = total_ref[1 - core].astype(BF16)


def orthogonal_rows(parts, rows):
    square = sum(jnp.sum(part * part, axis=(0, 1), keepdims=True) for part in parts)
    norm = jnp.sqrt(square) + 1e-07
    current = [(part / norm).astype(BF16) for part in parts]
    for iteration in range(ITERS):
        gram = sum(dot_columns(part, part) for part in current).astype(BF16)
        poly = (coef_two * gram.astype(F32) + coef_three * dot(gram, gram)).astype(BF16)
        if iteration == ITERS - 1:
            poly = poly[:rows]
            return [
                (coef_one * part[:rows].astype(F32) + dot(poly, part)).astype(BF16)
                for part in current
            ]
        current = [
            (coef_one * part.astype(F32) + dot(poly, part)).astype(BF16) for part in current
        ]


def stacked_parts(own, other, extent, window):
    return [
        jnp.concatenate([group[i][:extent, window] for i in order], axis=0).astype(F32)
        for group, order in ((own, (0, 1, 2, 3)), (other, (0, 2, 1, 3)))
    ]


def first_muon_kernel(place_ref, *refs):
    groups = [refs[4 * index : 4 * index + 4] for index in range(4)]
    moment_ref, orders_ref, early_ref, late_ref, sums_ref = refs[16:21]
    keep_ref, give_ref, new_moment_ref, bias_ref = refs[21:]
    core = place_ref[0]
    features = orders_ref.shape[0]
    rows = moment_ref.shape[0]
    quarter = features // 4
    wide = groups[0][0].shape[1]
    half = moment_ref.shape[1]

    messages = jnp.concatenate([ref[quarter:, :] for ref in groups[0] + groups[1]], axis=0)
    early = dot(early_ref[...], messages).astype(BF16)
    late = dot(late_ref[...], messages).astype(BF16)
    rest = 6 * features - wide
    modes = jnp.concatenate([early, late[:, :rest]], axis=1)
    act = dot(late[:, rest : rest + features], orders_ref[:, :features]).astype(BF16)
    sums = dot(sums_ref[...], late[:, rest + features :])
    bias_ref[:, : 6 * features] = column_sum(modes.astype(F32))
    samples = sums_ref.shape[0] - 4
    extent = (bias_ref.shape[1] - 6 * features) // samples
    for index in range(samples):
        start = 6 * features + index * extent
        bias_ref[:, start : start + extent] = sums[index : index + 1, :extent]
    modes_here = jnp.where(core == 0, modes[:, :half], modes[:, half:])
    part = dot_rows(act[:, :rows], modes_here)
    new_moment_ref[...] = momentum_decay * moment_ref[...] + part

    keep_ref[...] = jnp.zeros_like(keep_ref)
    give_ref[...] = jnp.zeros_like(give_ref)

    @pl.when(core == 0)
    def _():
        grown = 1.0 + momentum_decay
        moments = stacked_parts(groups[2], groups[3], quarter, slice(0, half))
        update = [
            grown * dot_rows(act, modes[:, side * half : (side + 1) * half])
            + momentum_decay**2 * moments[side]
            for side in range(2)
        ]
        keep, give = orthogonal_rows(update, rows)
        keep_ref[:, :half] = keep
        give_ref[:, :half] = give

    @pl.when(core == 1)
    def _():
        for member in range(2):
            window = slice(2 * member * features, 2 * (member + 1) * features)
            parts = stacked_parts(groups[0], groups[1], quarter, window)
            keep, give = orthogonal_rows(parts, rows)
            keep_ref[:, window] = keep
            give_ref[:, window] = give


def second_muon_kernel(place_ref, *refs):
    groups = [refs[4 * index : 4 * index + 4] for index in range(4)]
    keep_ref, give_ref = refs[16:]
    core = place_ref[0]
    rows = keep_ref.shape[0]
    quarter = groups[2][0].shape[0]
    wide = groups[0][0].shape[1]
    proj = wide - 16 * quarter
    keep_ref[...] = jnp.zeros_like(keep_ref)
    give_ref[...] = jnp.zeros_like(give_ref)

    @pl.when(core == 0)
    def _():
        parts = stacked_parts(groups[2], groups[3], quarter, slice(0, keep_ref.shape[1]))
        keep, give = orthogonal_rows(parts, rows)
        keep_ref[...] = keep
        give_ref[...] = give

    @pl.when(core == 1)
    def _():
        parts = stacked_parts(groups[0], groups[1], quarter, slice(wide - proj, wide))
        keep, give = orthogonal_rows(parts, rows)
        keep_ref[:, :proj] = keep
        give_ref[:, :proj] = give


def whole(shape):
    return pl.BlockSpec(shape, lambda index: (0,) * len(shape))


def each(shape, start=0):
    return pl.BlockSpec(
        (1,) + tuple(shape[1:]), lambda index: (index + start,) + (0,) * (len(shape) - 1)
    )


SMEM_WHOLE = pl.BlockSpec(memory_space=pltpu.SMEM)


def cost(flops):
    return pl.CostEstimate(flops=flops, bytes_accessed=2**20, transcendentals=0)


def run_whole(kernel, place, operands, results, flops):
    vmem = pl.BlockSpec(memory_space=pltpu.VMEM)
    return pl.pallas_call(
        kernel,
        in_specs=[SMEM_WHOLE] + [vmem] * len(operands),
        out_shape=results,
        compiler_params=pltpu.CompilerParams(vmem_limit_bytes=56 * 2**20),
        cost_estimate=cost(flops),
    )(place, *operands)


def run_mix(x, modes, bias, wqkv):
    samples, length, features = x.shape
    results = [
        struct((samples, length, features), BF16),
        struct((samples, length, 3 * features), BF16),
        struct((samples, length, 128), F32),
        struct((samples, length, features), BF16),
    ]
    return pl.pallas_call(
        mix_kernel,
        grid=(samples,),
        in_specs=[each(x.shape), each(modes.shape), whole(bias.shape), whole(wqkv.shape)],
        out_specs=[each(member.shape) for member in results],
        out_shape=results,
        compiler_params=params(),
        cost_estimate=cost(samples * length * features * 30000),
    )(x, modes, bias, wqkv)


def run_hidden(place, counts, own, other, x, cot, mixed, modes, bias, orders):
    samples, length, features = x.shape
    wide = own[0].shape[1]
    hidden = 4 * features
    results = [
        struct((samples, length, features), BF16),
        struct((samples, length, features), BF16),
        struct((samples, length, features), F32),
        struct((samples, 1, 6 * features), F32),
        struct((1, 2 * features + hidden), F32),
        struct((features, wide), F32),
        struct((features, wide), BF16),
    ]
    return pl.pallas_call(
        hidden_kernel,
        grid=(samples,),
        in_specs=[SMEM_WHOLE, SMEM_WHOLE]
        + [whole(piece.shape) for piece in own + other]
        + [each(x.shape), each(cot.shape), each(mixed.shape), each(modes.shape)]
        + [whole(bias.shape), whole(orders.shape)],
        out_specs=[each(member.shape) for member in results[:4]]
        + [whole(member.shape) for member in results[4:]],
        out_shape=results,
        scratch_shapes=[
            pltpu.VMEM((2, features, wide), F32),
            pltpu.VMEM((features, hidden), BF16),
            pltpu.VMEM((features, hidden), BF16),
            pltpu.VMEM((features, features), BF16),
        ],
        compiler_params=params(),
        cost_estimate=cost(samples * length * features * 60000),
    )(place, counts, *own, *other, x, cot, mixed, modes, bias, orders)


def run_scores(start, count, qkv, lse, dmix):
    features = dmix.shape[-1]
    length = dmix.shape[-2]
    return pl.pallas_call(
        scores_kernel,
        grid=(count,),
        in_specs=[each(member.shape, start) for member in (qkv, lse, dmix)],
        out_specs=each(qkv.shape),
        out_shape=struct((count,) + qkv.shape[1:], BF16),
        compiler_params=params(),
        cost_estimate=cost(count * length * features * 30000),
    )(qkv, lse, dmix)


def run_closing(place, starts, parts, operands, wqkv, orders):
    samples, length, features = operands[0].shape
    padded = (3 * features // 2 + 127) // 128 * 128
    results = [
        struct((samples, length, features), F32),
        struct((samples, 1, 6 * features), BF16),
        struct((1, 2 * features), F32),
        struct((features, padded), F32),
        struct((features, padded), BF16),
    ]

    def part_spec(start, part):
        last = part.shape[0] - 1
        return pl.BlockSpec(
            (1,) + part.shape[1:], lambda index: (jnp.clip(index - start, 0, last), 0, 0)
        )

    return pl.pallas_call(
        functools.partial(closing_kernel, starts),
        grid=(samples,),
        in_specs=[SMEM_WHOLE]
        + [part_spec(start, part) for start, part in zip(starts, parts)]
        + [each(member.shape) for member in operands]
        + [whole(wqkv.shape), whole(orders.shape)],
        out_specs=[each(member.shape) for member in results[:2]]
        + [whole(member.shape) for member in results[2:]],
        out_shape=results,
        scratch_shapes=[pltpu.VMEM((2, features, padded), F32)],
        compiler_params=params(),
        cost_estimate=cost(samples * length * features * 20000),
    )(place, *parts, *operands, wqkv, orders)


def local(
    latents,
    conditions,
    counts,
    cotangent,
    w_ada,
    w_qkv,
    w_proj,
    w_fc1,
    w_fc2,
    biases,
    m_ada,
    m_qkv,
    m_proj,
    m_fc1,
    m_fc2,
    bias_first,
    bias_second,
):
    links = Links()
    core = links.core
    batches, slots, length, features = latents.shape
    samples = batches * slots
    rows = w_ada.shape[0]
    hidden = 2 * w_fc1.shape[1]
    plain = rows % 8 > 0
    half_ada, half_qkv, half_proj = w_ada.shape[1], w_qkv.shape[1], w_proj.shape[1]
    half_fc = hidden // 2
    wide = half_ada + (half_qkv + 127) // 128 * 128
    devices = 2 * links.groups

    def tie(value, other):
        return lax.optimization_barrier((value, other))[0]

    place = jnp.stack([core, links.me]).astype(jnp.int32)

    bias_here = biases.shape[0]
    bias_columns = bias_here // rows
    padded_qkv = wide - half_ada - half_qkv
    padded_proj = wide - hidden - half_proj

    def pack(*pieces):
        empty = jnp.zeros((rows, wide - sum(piece.shape[1] for piece in pieces)), F32)
        return jnp.concatenate(list(pieces) + [empty], axis=1).astype(BF16)

    block_first = fused(pack, w_ada, w_qkv, biases.reshape(rows, bias_columns), plain=plain)
    block_rest, block_moment = fused(
        lambda fc1, fc2, proj, moment: (pack(fc1, fc2, proj), moment.astype(BF16)),
        w_fc1,
        w_fc2.T,
        w_proj,
        m_ada,
        plain=plain,
    )
    first_held = links.gather_far(block_first, rows)
    first_own = links.gather_near(first_held)
    first_other = links.swap_pairs(first_own)
    rest_held = links.gather_far(tie(block_rest, first_held), rows)
    rest_own = links.gather_near(rest_held)
    rest_other = links.swap_pairs(rest_own)

    orders = jnp.concatenate([links.order(0, rows), links.order(1, rows)], axis=1)
    line_places = jnp.concatenate(
        [links.bias_places(side, rows, bias_columns, (1, features), 1) for side in range(2)],
        axis=0,
    )
    lane_places = jnp.concatenate(
        [links.bias_places(side, rows, bias_columns, (features, 128), 0) for side in range(2)],
        axis=1,
    )
    conditions_flat = conditions.reshape(samples, features)
    qkv_full, bias_all, modes, cond_act = run_whole(
        modes_kernel,
        place,
        first_own + first_other + [conditions_flat, orders, line_places, lane_places],
        [
            struct((features, 3 * features), BF16),
            struct((1, bias_here * devices), F32),
            struct((samples, 1, 6 * features), F32),
            struct((samples, features), BF16),
        ],
        2 * 10**9,
    )

    x = latents.reshape(samples, length, features)
    cot = cotangent.reshape(samples, length, features)
    block_moment = tie(block_moment, rest_held)
    attn_in, qkv, log_totals, mixed = run_mix(x, modes, bias_all, qkv_full)
    moment_held = links.gather_far(block_moment, rows)
    mixed = tie(mixed, moment_held)
    block_out, grad_mixed, grad_after, first_modes, bias_rest_sum, mine_rest, give_rest = run_hidden(
        place, counts, rest_own, rest_other, x, cot, mixed, modes, bias_all, orders
    )
    moment_own = links.gather_near(moment_held)
    rest_steps = links.scatter(mine_rest, give_rest, False)
    starts = (0, 1, samples - 1)
    counts_here = (1, samples - 2, 1)
    parts = []
    grad_mixed = tie(grad_mixed, moment_own[3])
    kept_rest, arrived_rest = None, None
    for start, count in zip(starts, counts_here):
        part = run_scores(start, count, qkv, log_totals, grad_mixed)
        parts.append(part)
        kept_rest, arrived_rest = next(rest_steps)
        grad_mixed, kept_rest = lax.optimization_barrier((grad_mixed, kept_rest))
    grad_after = tie(grad_after, kept_rest)
    moment_other = links.swap_pairs(moment_own)
    grad_latent, grad_modes, bias_qkv_sum, mine_qkv, give_qkv = run_closing(
        place,
        starts,
        parts,
        [x, grad_after, modes, attn_in, first_modes],
        qkv_full,
        orders,
    )
    for kept_rest, arrived_rest in rest_steps:
        pass
    for kept_qkv, arrived_qkv in links.scatter(mine_qkv, give_qkv, True):
        pass

    def stepped(kept, arrived, moment):
        for piece in arrived:
            kept = kept + piece.astype(F32)
        new_moment = momentum_decay * moment + kept
        return new_moment, kept + momentum_decay * new_moment

    later = 6 * features - wide

    def update_rest(kept, one, two, three, fc1, fc2, proj, grads, act, bias_qkv, bias_rest):
        empty = jnp.zeros((rows, padded_proj), F32)
        moment = jnp.concatenate([fc1, fc2, proj, empty], axis=1)
        new_moment, direction = stepped(kept, [one, two, three], moment)
        bias_flat = jnp.concatenate([bias_qkv, bias_rest], axis=1)
        share = bias_flat.shape[1] // samples
        row = lax.broadcasted_iota(jnp.int32, (2 * samples, wide), 0)
        message = jnp.zeros((2 * samples, wide), F32)
        for index in range(samples):
            grad = grads[index].astype(F32)
            late = jnp.concatenate(
                [
                    grad[:, wide:],
                    act[index : index + 1].astype(F32),
                    bias_flat[:, index * share : (index + 1) * share],
                    jnp.zeros((1, wide - later - features - share), F32),
                ],
                axis=1,
            )
            message = jnp.where(row == index, grad[:, :wide], message)
            message = jnp.where(row == samples + index, late, message)
        block = jnp.concatenate([direction, message], axis=0).astype(BF16)
        return (
            new_moment[:, :half_fc],
            new_moment[:, half_fc:hidden],
            new_moment[:, hidden : hidden + half_proj],
            block,
        )

    def total_of(arrived):
        while len(arrived) < 3:
            arrived = arrived + [jnp.zeros_like(arrived[0])]
        return arrived

    new_fc1, new_fc2, new_proj, update_block = fused(
        update_rest,
        kept_rest,
        *total_of(arrived_rest),
        m_fc1,
        m_fc2.T,
        m_proj,
        grad_modes,
        cond_act,
        bias_qkv_sum,
        bias_rest_sum,
        plain=plain,
    )
    update_own = links.gather_near(links.gather_far(update_block, rows))
    update_other = links.swap_pairs(update_own)

    def update_qkv(kept, one, two, three, moment):
        moment = jnp.concatenate([moment, jnp.zeros((rows, padded_qkv), F32)], axis=1)
        new_moment, direction = stepped(kept, [one, two, three], moment)
        return new_moment[:, :half_qkv], direction.astype(BF16)

    new_qkv, qkv_block = fused(
        update_qkv,
        kept_qkv,
        *total_of(arrived_qkv),
        m_qkv,
        plain=plain,
    )
    qkv_own = links.gather_direct(links.gather_far(qkv_block, rows))
    qkv_other = links.swap_pairs(qkv_own)
    grad_conditions = run_whole(
        condition_kernel,
        place,
        first_own + first_other + [grad_modes, conditions_flat, orders],
        struct((samples, features), F32),
        10**9,
    )

    message_rows = 2 * samples * devices
    row = lax.broadcasted_iota(jnp.int32, (samples * devices, message_rows), 0)
    column = lax.broadcasted_iota(jnp.int32, (samples * devices, message_rows), 1)
    source = row // samples * 2 * samples + row % samples
    early_pick = (column == source).astype(BF16)
    late_pick = (column == source + samples).astype(BF16)
    row = lax.broadcasted_iota(jnp.int32, (samples + 4, samples * devices), 0)
    column = lax.broadcasted_iota(jnp.int32, (samples + 4, samples * devices), 1)
    sums_pick = (column % samples == row).astype(BF16)
    keep_first, give_first, new_ada, bias_sum = run_whole(
        first_muon_kernel,
        place,
        update_own
        + update_other
        + moment_own
        + moment_other
        + [m_ada, orders, early_pick, late_pick, sums_pick],
        [
            struct((rows, hidden), BF16),
            struct((rows, hidden), BF16),
            struct((rows, half_ada), F32),
            struct((1, bias_here * devices), F32),
        ],
        10**10,
    )
    keep_second, give_second = run_whole(
        second_muon_kernel,
        place,
        update_own + update_other + qkv_own + qkv_other,
        [struct((rows, wide - half_ada), BF16), struct((rows, wide - half_ada), BF16)],
        3 * 10**9,
    )
    taken_first = links.swap_pair(give_first)
    taken_second = links.swap_pair(give_second)
    factors = [math.sqrt(max(1.0, aspect)) for aspect in (6.0, 3.0, 1.0, 4.0, 0.25)]

    def finish(keep_first, taken_first, keep_second, taken_second, core, ada, qkv, proj, fc1, fc2):
        kept = [value.astype(F32) for value in (keep_first, keep_second)]
        taken = [value.astype(F32) for value in (taken_first, taken_second)]
        zero = [jnp.where(core == 0, one, other) for one, other in zip(kept, taken)]
        one = [jnp.where(core == 0, other, one) for one, other in zip(kept, taken)]
        parts = (
            zero[0][:, :half_ada],
            zero[1][:, :half_qkv],
            one[1][:, :half_proj],
            one[0][:, :half_fc],
            one[0][:, half_fc:hidden],
        )
        return [
            master * (1.0 - matrix_rate * decay_rate) - matrix_rate * factor * part
            for master, factor, part in zip((ada, qkv, proj, fc1, fc2), factors, parts)
        ]

    new_weights = fused(
        finish,
        keep_first,
        taken_first,
        keep_second,
        taken_second,
        jnp.broadcast_to(core.astype(jnp.int32), (1, 1)),
        w_ada,
        w_qkv,
        w_proj,
        w_fc1,
        w_fc2.T,
        plain=plain,
    )
    bias_grad = lax.dynamic_slice(
        bias_sum.reshape(-1), ((2 * links.me + core) * bias_here,), (bias_here,)
    )
    first_new = first_decay * bias_first + (1.0 - first_decay) * bias_grad
    second_new = second_decay * bias_second + (1.0 - second_decay) * bias_grad * bias_grad
    first_fix = 1.0 - first_decay**STEP
    second_fix = 1.0 - second_decay**STEP
    bias_new = biases * (1.0 - bias_rate * decay_rate) - bias_rate * (first_new / first_fix) / (
        jnp.sqrt(second_new / second_fix) + 1e-08
    )
    shape = (batches, slots, length, features)
    return (
        block_out.reshape(shape),
        grad_latent.reshape(shape),
        grad_conditions.reshape(batches, slots, features),
        new_ada,
        new_qkv,
        new_proj,
        new_fc1,
        new_fc2.T,
        new_weights[0],
        new_weights[1],
        new_weights[2],
        new_weights[3],
        new_weights[4].T,
        bias_grad,
        second_new,
        bias_new,
    )


def solution(mesh):
    samples = P(None, AXES, None, None)
    matrix = P("dp", "pair")
    turned = P("pair", "dp")
    vector = P(AXES)
    conditions = P(None, AXES, None)
    in_specs = (
        (samples, conditions, P(None, AXES), samples)
        + (matrix, matrix, matrix, matrix, turned, vector)
        + (matrix, matrix, matrix, matrix, turned, vector, vector)
    )
    out_specs = (
        (samples, samples, conditions)
        + (matrix, matrix, matrix, matrix, turned)
        + (matrix, matrix, matrix, matrix, turned)
        + (vector, vector, vector)
    )
    return jax.shard_map(local, mesh=mesh, in_specs=in_specs, out_specs=out_specs, check_vma=False)
```

profile of v0, /device:TPU:0, one launch (start us, length us, event | category | flops | bytes accessed | tf_op | source)
XLA Modules:
  0.0 286.8 jit_solution(13869717631751723068)
XLA Ops:
  3.7 3.0 %collective-permute-start = (bf16[24,1792]{1,0:T(8,128)(2,1)}, bf16[24,1792]{1,0:T(8,128)(2,1)S(1)}, u32[]{:S(2)}, u32[]{:S(2)}) collective-permute-start(bf16[24,1792]{1,0:T(8,128)(2,1)} %shard_map.289.refs_0_), channel_id=1, source_target_pairs={{0,8},{1,9},{2,10},{3,11},{4,12},{5,13},{6,14},{7,15},{8,0},{9,1},... | collective-permute-start | bytes 258056 | tf_op jit(solution)/shard_map/ppermute | solution.py:104
  6.7 2.6 collective-permute-start.1
  11.0 5.4 %collective-permute-done.1.refs_2_ = bf16[24,1792]{1,0:T(8,128)(2,1)S(1)} collective-permute-done((bf16[24,1792]{1,0:T(8,128)(2,1)}, bf16[24,1792]{1,0:T(8,128)(2,1)S(1)}, u32[]{:S(2)}, u32[]{:S(2)}) %collective-permute-start.1) | collective-permute-done | bytes 86048 | tf_op jit(solution)/shard_map/ppermute | solution.py:104
  17.7 1.8 shard_map.290.refs_0_
  21.9 2.2 collective-permute-start.4
  27.5 1.8 collective-permute-done.4.refs_2_
  37.1 3.0 %collective-permute-done.20.refs_1_ = bf16[24,1152]{1,0:T(8,128)(2,1)S(1)} collective-permute-done((bf16[24,1152]{1,0:T(8,128)(2,1)S(1)}, bf16[24,1152]{1,0:T(8,128)(2,1)S(1)}, u32[]{:S(2)}, u32[]{:S(2)}) %collective-permute-start.20) | collective-permute-done | bytes 55328 | tf_op jit(solution)/shard_map/ppermute | solution.py:104
  40.0 1.8 collective-permute-start.21
  42.4 4.2 %collective-permute-done.21.refs_2_ = bf16[24,1152]{1,0:T(8,128)(2,1)S(1)} collective-permute-done((bf16[24,1152]{1,0:T(8,128)(2,1)S(1)}, bf16[24,1152]{1,0:T(8,128)(2,1)S(1)}, u32[]{:S(2)}, u32[]{:S(2)}) %collective-permute-start.21) | collective-permute-done | bytes 55328 | tf_op jit(solution)/shard_map/ppermute | solution.py:104
  46.6 2.6 collective-permute-start.22
  52.5 1.8 collective-permute-start.7
  60.6 3.1 %collective-permute-done.8.refs_3_ = bf16[96,1792]{1,0:T(8,128)(2,1)S(1)} collective-permute-done((bf16[96,1792]{1,0:T(8,128)(2,1)S(1)}, bf16[96,1792]{1,0:T(8,128)(2,1)S(1)}, u32[]{:S(2)}, u32[]{:S(2)}) %collective-permute-start.8) | collective-permute-done | bytes 344096 | tf_op jit(solution)/shard_map/ppermute | solution.py:104
  64.5 4.4 %shard_map.292 = (bf16[384,1152]{1,0:T(8,128)(2,1)}, f32[1,5376]{1,0:T(1,128)}, f32[4,1,2304]{2,1,0:T(1,128)}, bf16[4,384]{1,0:T(4,128)(2,1)}) custom-call(s32[2]{0:T(128)} %pad_add_fusion.2.place_ref, bf16[96,1792]{1,0:T(8,128)(2,1)} %shard_map.290.refs_0_, bf16[96,1792]{1,0:T(8,128)(2,1)} %copy-done.46, bf16[96,1792]{1,0:T(8,128)(2,1)} %copy-done.47, ...), custom_call_target="tpu_custom_call" | custom-call | flops 2000000000 | bytes 1048576 | tf_op jit(solution)/shard_map/pallas_call | solution.py:610
  68.9 8.7 %shard_map.293 = (bf16[4,256,384]{2,1,0:T(8,128)(2,1)}, bf16[4,256,1152]{2,1,0:T(8,128)(2,1)}, f32[4,256,128]{2,1,0:T(8,128)}, bf16[4,256,384]{2,1,0:T(8,128)(2,1)}) custom-call(bf16[4,256,384]{2,1,0:T(8,128)(2,1)} %bitcast.18, f32[4,1,2304]{2,1,0:T(1,128)} %get-tuple-element.81.modes_ref.refs_11_.refs_5_, f32[1,5376]{1,0:T(1,128)} %get-tuple-element.82.bias_ref.refs_12_, ...), custom_call_target="tpu_custom_call" | custom-call | flops 11796480000 | bytes 1048576 | tf_op jit(solution)/shard_map/pallas_call | solution.py:627
  78.7 29.0 %shard_map.295 = (bf16[4,256,384]{2,1,0:T(8,128)(2,1)}, bf16[4,256,384]{2,1,0:T(8,128)(2,1)}, f32[4,256,384]{2,1,0:T(8,128)}, f32[4,1,2304]{2,1,0:T(1,128)}, f32...) custom-call(s32[2]{0:T(128)} %pad_add_fusion.2.place_ref, s32[2,1]{1,0:T(2,128)} %copy.34.counts_ref, ...), custom_call_target="tpu_custom_call" | custom-call | flops 23592960000 | bytes 1048576 | tf_op jit(solution)/shard_map/pallas_call | solution.py:651
  109.1 2.0 collective-permute-done.25.refs_1_
  112.3 3.6 %shard_map.297 = (f32[192,1792]{1,0:T(8,128)}, bf16[192,1792]{1,0:T(8,128)(2,1)}) custom-call(f32[384,1792]{1,0:T(8,128)} %get-tuple-element.93.refs_0_, bf16[384,1792]{1,0:T(8,128)(2,1)} %copy-done), custom_call_target="tpu_custom_call" | custom-call | bytes 8257536 | tf_op jit(solution)/shard_map/pallas_call | solution.py:77
  115.8 1.8 collective-permute-start.26
  117.9 11.5 %collective-permute-done.24.refs_11_ = bf16[96,1152]{1,0:T(8,128)(2,1)S(1)} collective-permute-done((bf16[96,1152]{1,0:T(8,128)(2,1)S(1)}, bf16[96,1152]{1,0:T(8,128)(2,1)S(1)}, u32[]{:S(2)}, u32[]{:S(2)}) %collective-permute-start.24) | collective-permute-done | bytes 221216 | tf_op jit(solution)/shard_map/ppermute | solution.py:104
  129.4 4.7 %shard_map.296.refs_0_ = bf16[1,256,1152]{2,1,0:T(8,128)(2,1)} custom-call(bf16[4,256,1152]{2,1,0:T(8,128)(2,1)} %get-tuple-element.89.qkv_ref, f32[4,256,128]{2,1,0:T(8,128)} %get-tuple-element.90.lse_ref, bf16[4,256,384]{2,1,0:T(8,128)(2,1)} %get-tuple-element.99.dmix_ref), custom_call_target="tpu_custom_call" | custom-call | flops 2949120000 | bytes 1048576 | tf_op jit(solution)/shard_map/pallas_call | solution.py:675
  134.9 2.6 shard_map.299
  138.4 7.4 %shard_map.298.refs_1_ = bf16[2,256,1152]{2,1,0:T(8,128)(2,1)} custom-call(bf16[4,256,1152]{2,1,0:T(8,128)(2,1)} %get-tuple-element.89.qkv_ref, f32[4,256,128]{2,1,0:T(8,128)} %get-tuple-element.90.lse_ref, bf16[4,256,384]{2,1,0:T(8,128)(2,1)} %get-tuple-element.99.dmix_ref), custom_call_target="tpu_custom_call" | custom-call | flops 5898240000 | bytes 1048576 | tf_op jit(solution)/shard_map/pallas_call | solution.py:675
  145.8 4.7 %shard_map.300.refs_2_ = bf16[1,256,1152]{2,1,0:T(8,128)(2,1)} custom-call(bf16[4,256,1152]{2,1,0:T(8,128)(2,1)} %get-tuple-element.89.qkv_ref, f32[4,256,128]{2,1,0:T(8,128)} %get-tuple-element.90.lse_ref, bf16[4,256,384]{2,1,0:T(8,128)(2,1)} %get-tuple-element.99.dmix_ref), custom_call_target="tpu_custom_call" | custom-call | flops 2949120000 | bytes 1048576 | tf_op jit(solution)/shard_map/pallas_call | solution.py:675
  151.2 1.9 shard_map.301
  153.2 9.2 %shard_map.302 = (f32[4,256,384]{2,1,0:T(8,128)}, bf16[4,1,2304]{2,1,0:T(2,128)(2,1)}, f32[1,768]{1,0:T(1,128)}, f32[384,640]{1,0:T(8,128)}, bf16[384,640]{1,0:T(8,128)(2,1)}) custom-call(s32[2]{0:T(128)} %pad_add_fusion.2.place_ref, bf16[1,256,1152]{2,1,0:T(8,128)(2,1)} %shard_map.296.refs_0_, bf16[2,256,1152]{2,1,0:T(8,128)(2,1)} %shard_map.298.refs_1_, ...), custom_call_target="tpu_custom_call" | custom-call | flops 7864320000 | bytes 1048576 | tf_op jit(solution)/shard_map/pallas_call | solution.py:703
  162.6 2.5 collective-permute-start.29
  165.1 1.9 collective-permute-start.30
  168.6 4.1 %collective-permute-done.29.refs_2_ = bf16[24,1792]{1,0:T(8,128)(2,1)S(1)} collective-permute-done((bf16[24,1792]{1,0:T(8,128)(2,1)S(1)}, bf16[24,1792]{1,0:T(8,128)(2,1)S(1)}, u32[]{:S(2)}, u32[]{:S(2)}) %collective-permute-start.29) | collective-permute-done | bytes 86048 | tf_op jit(solution)/shard_map/ppermute | solution.py:104
  173.3 1.9 shard_map.304
  175.3 1.8 collective-permute-start.31
  177.8 1.9 collective-permute-start.33
  181.0 7.3 %collective-permute-done.32.refs_2_ = bf16[32,1792]{1,0:T(8,128)(2,1)S(1)} collective-permute-done((bf16[32,1792]{1,0:T(8,128)(2,1)}, bf16[32,1792]{1,0:T(8,128)(2,1)S(1)}, u32[]{:S(2)}, u32[]{:S(2)}) %collective-permute-start.32) | collective-permute-done | bytes 114720 | tf_op jit(solution)/shard_map/ppermute | solution.py:104
  189.6 1.9 shard_map.305.refs_0_
  195.5 2.2 shard_map.307
  198.5 2.7 collective-permute-start.49
  201.1 6.6 %collective-permute-done.47.refs_1_ = bf16[96,640]{1,0:T(8,128)(2,1)S(1)} collective-permute-done((bf16[96,640]{1,0:T(8,128)(2,1)}, bf16[96,640]{1,0:T(8,128)(2,1)S(1)}, u32[]{:S(2)}, u32[]{:S(2)}) %collective-permute-start.47) | collective-permute-done | bytes 122912 | tf_op jit(solution)/shard_map/ppermute | solution.py:104
  208.5 1.8 shard_map.308
  210.3 3.2 %collective-permute-start.50 = (bf16[24,640]{1,0:T(8,128)(2,1)}, bf16[24,640]{1,0:T(8,128)(2,1)S(1)}, u32[]{:S(2)}, u32[]{:S(2)}) collective-permute-start(bf16[24,640]{1,0:T(8,128)(2,1)} %get-tuple-element.124), channel_id=1, source_target_pairs={{0,8},{1,9},{2,10},{3,11},{4,12},{5,13},{6,14},{7,15},{8,0},{9,1},... | collective-permute-start | bytes 92168 | tf_op jit(solution)/shard_map/ppermute | solution.py:104
  216.2 2.8 collective-permute-done.51.refs_2_
  225.1 1.8 collective-permute-done.54.refs_1_
  227.1 4.8 %collective-permute-done.55.refs_2_ = bf16[24,640]{1,0:T(8,128)(2,1)S(1)} collective-permute-done((bf16[24,640]{1,0:T(8,128)(2,1)}, bf16[24,640]{1,0:T(8,128)(2,1)S(1)}, u32[]{:S(2)}, u32[]{:S(2)}) %collective-permute-start.55) | collective-permute-done | bytes 30752 | tf_op jit(solution)/shard_map/ppermute | solution.py:104
  233.4 4.5 %collective-permute-done.56.refs_3_ = bf16[24,640]{1,0:T(8,128)(2,1)S(1)} collective-permute-done((bf16[24,640]{1,0:T(8,128)(2,1)}, bf16[24,640]{1,0:T(8,128)(2,1)S(1)}, u32[]{:S(2)}, u32[]{:S(2)}) %collective-permute-start.56) | collective-permute-done | bytes 30752 | tf_op jit(solution)/shard_map/ppermute | solution.py:104
  246.2 2.0 collective-permute-done.59.refs_11_
  251.4 4.6 %shard_map.303 = f32[4,384]{1,0:T(4,128)} custom-call(s32[2]{0:T(128)} %pad_add_fusion.2.place_ref, bf16[96,1792]{1,0:T(8,128)(2,1)} %shard_map.290.refs_0_, bf16[96,1792]{1,0:T(8,128)(2,1)} %copy-done.46, bf16[96,1792]{1,0:T(8,128)(2,1)} %copy-done.47, bf16[96,1792]{1,0:T(8,128)(2,1)} %copy-done.49, bf16[96,1792]{1,0:T(8,128)(2,1)} %copy-done.48, ...), custom_call_target="tpu_custom_call" | custom-call | flops 1000000000 | bytes 1048576 | tf_op jit(solution)/shard_map/pallas_call | solution.py:610
  259.6 7.6 %shard_map.311 = (bf16[24,640]{1,0:T(8,128)(2,1)}, bf16[24,640]{1,0:T(8,128)(2,1)}) custom-call(s32[2]{0:T(128)} %pad_add_fusion.2.place_ref, bf16[128,1792]{1,0:T(8,128)(2,1)} %shard_map.305.refs_0_, bf16[128,1792]{1,0:T(8,128)(2,1)} %copy-done.39, bf16[128,1792]{1,0:T(8,128)(2,1)} %copy-done.40, bf16[128,1792]{1,0:T(8,128)(2,1)} %copy-done.42, ...), custom_call_target="tpu_custom_call" | custom-call | flops 3000000000 | bytes 1048576 | tf_op jit(solution)/shard_map/pallas_call | solution.py:610
  268.2 12.1 %shard_map.306 = (bf16[24,1536]{1,0:T(8,128)(2,1)}, bf16[24,1536]{1,0:T(8,128)(2,1)}, f32[24,1152]{1,0:T(8,128)}, f32[1,5376]{1,0:T(1,128)}) custom-call(s32[2]{0:T(128)} %pad_add_fusion.2.place_ref, bf16[128,1792]{1,0:T(8,128)(2,1)} %shard_map.305.refs_0_, bf16[128,1792]{1,0:T(8,128)(2,1)} %copy-done.39, bf16[128,1792]{1,0:T(8,128)(2,1)} %copy-done.40, ...), custom_call_target="tpu_custom_call" | custom-call | flops 10000000000 | bytes 1048576 | tf_op jit(solution)/shard_map/pallas_call | solution.py:610
  280.3 2.4 collective-permute-start.53
  284.6 1.9 shard_map.312
  (277 shorter events, 76.3 us)
Async XLA Ops:
  3.7 7.3 %collective-permute-start = (bf16[24,1792]{1,0:T(8,128)(2,1)}, bf16[24,1792]{1,0:T(8,128)(2,1)S(1)}, u32[]{:S(2)}, u32[]{:S(2)}) collective-permute-start(bf16[24,1792]{1,0:T(8,128)(2,1)} %shard_map.289.refs_0_), channel_id=1, source_target_pairs={{0,8},{1,9},{2,10},{3,11},{4,12},{5,13},{6,14},{7,15},{8,0},{9,1},... | collective-permute-start | bytes 258056 | tf_op jit(solution)/shard_map/ppermute | solution.py:104
  6.7 9.7 %collective-permute-start.1 = (bf16[24,1792]{1,0:T(8,128)(2,1)}, bf16[24,1792]{1,0:T(8,128)(2,1)S(1)}, u32[]{:S(2)}, u32[]{:S(2)}) collective-permute-start(bf16[24,1792]{1,0:T(8,128)(2,1)} %shard_map.289.refs_0_), channel_id=1, source_target_pairs={{0,16},{1,17},{2,18},{3,19},{4,20},{5,21},{6,22},{7,23},{8,24},{9,... | collective-permute-start | bytes 258056 | tf_op jit(solution)/shard_map/ppermute | solution.py:104
  9.3 7.1 %collective-permute-start.2 = (bf16[24,1792]{1,0:T(8,128)(2,1)}, bf16[24,1792]{1,0:T(8,128)(2,1)S(1)}, u32[]{:S(2)}, u32[]{:S(2)}) collective-permute-start(bf16[24,1792]{1,0:T(8,128)(2,1)} %shard_map.289.refs_0_), channel_id=1, source_target_pairs={{0,24},{1,25},{2,26},{3,27},{4,28},{5,29},{6,30},{7,31},{8,16},{9,... | collective-permute-start | bytes 258056 | tf_op jit(solution)/shard_map/ppermute | solution.py:104
  19.5 15.3 %collective-permute-start.13 = (bf16[96,1792]{1,0:T(8,128)(2,1)}, bf16[96,1792]{1,0:T(8,128)(2,1)S(1)}, u32[]{:S(2)}, u32[]{:S(2)}) collective-permute-start(bf16[96,1792]{1,0:T(8,128)(2,1)} %shard_map.290.refs_0_), channel_id=1, source_target_pairs={{0,4},{1,3},{2,6},{3,1},{4,0},{5,7},{6,2},{7,5},{8,12},{9,11},{10,... | collective-permute-start | bytes 1032200 | tf_op jit(solution)/shard_map/ppermute | solution.py:104
  21.0 6.5 %collective-permute-start.3 = (bf16[24,1792]{1,0:T(8,128)(2,1)}, bf16[24,1792]{1,0:T(8,128)(2,1)S(1)}, u32[]{:S(2)}, u32[]{:S(2)}) collective-permute-start(bf16[24,1792]{1,0:T(8,128)(2,1)} %get-tuple-element.80.refs_0_), channel_id=1, source_target_pairs={{0,8},{1,9},{2,10},{3,11},{4,12},{5,13},{6,14},{7,15},{8,0},{9,1},... | collective-permute-start | bytes 258056 | tf_op jit(solution)/shard_map/ppermute | solution.py:104
  21.9 7.5 %collective-permute-start.4 = (bf16[24,1792]{1,0:T(8,128)(2,1)}, bf16[24,1792]{1,0:T(8,128)(2,1)S(1)}, u32[]{:S(2)}, u32[]{:S(2)}) collective-permute-start(bf16[24,1792]{1,0:T(8,128)(2,1)} %get-tuple-element.80.refs_0_), channel_id=1, source_target_pairs={{0,16},{1,17},{2,18},{3,19},{4,20},{5,21},{6,22},{7,23},{8,24},{9,... | collective-permute-start | bytes 258056 | tf_op jit(solution)/shard_map/ppermute | solution.py:104
  24.1 6.6 %collective-permute-start.5 = (bf16[24,1792]{1,0:T(8,128)(2,1)}, bf16[24,1792]{1,0:T(8,128)(2,1)S(1)}, u32[]{:S(2)}, u32[]{:S(2)}) collective-permute-start(bf16[24,1792]{1,0:T(8,128)(2,1)} %get-tuple-element.80.refs_0_), channel_id=1, source_target_pairs={{0,24},{1,25},{2,26},{3,27},{4,28},{5,29},{6,30},{7,31},{8,16},{9,... | collective-permute-start | bytes 258056 | tf_op jit(solution)/shard_map/ppermute | solution.py:104
  26.0 28.4 %collective-permute-start.14 = (bf16[96,1792]{1,0:T(8,128)(2,1)}, bf16[96,1792]{1,0:T(8,128)(2,1)S(1)}, u32[]{:S(2)}, u32[]{:S(2)}) collective-permute-start(bf16[96,1792]{1,0:T(8,128)(2,1)} %shard_map.290.refs_0_), channel_id=1, source_target_pairs={{0,2},{1,5},{2,0},{3,7},{4,6},{5,1},{6,4},{7,3},{8,10},{9,13},{10,... | collective-permute-start | bytes 1032200 | tf_op jit(solution)/shard_map/ppermute | solution.py:104
  27.5 26.8 %collective-permute-start.16 = (bf16[96,1792]{1,0:T(8,128)(2,1)}, bf16[96,1792]{1,0:T(8,128)(2,1)S(1)}, u32[]{:S(2)}, u32[]{:S(2)}) collective-permute-start(bf16[96,1792]{1,0:T(8,128)(2,1)} %shard_map.290.refs_0_), channel_id=1, source_target_pairs={{0,1},{1,0},{2,3},{3,2},{4,5},{5,4},{6,7},{7,6},{8,9},{9,8},{10,11... | collective-permute-start | bytes 1032200 | tf_op jit(solution)/shard_map/ppermute | solution.py:107
  33.1 21.8 %collective-permute-start.6 = (bf16[96,1792]{1,0:T(8,128)(2,1)}, bf16[96,1792]{1,0:T(8,128)(2,1)S(1)}, u32[]{:S(2)}, u32[]{:S(2)}) collective-permute-start(bf16[96,1792]{1,0:T(8,128)(2,1)} %shard_map.291.refs_0_), channel_id=1, source_target_pairs={{0,4},{1,3},{2,6},{3,1},{4,0},{5,7},{6,2},{7,5},{8,12},{9,11},{10,... | collective-permute-start | bytes 1032200 | tf_op jit(solution)/shard_map/ppermute | solution.py:104
  34.8 20.3 %collective-permute-start.15 = (bf16[96,1792]{1,0:T(8,128)(2,1)S(1)}, bf16[96,1792]{1,0:T(8,128)(2,1)S(1)}, u32[]{:S(2)}, u32[]{:S(2)}) collective-permute-start(bf16[96,1792]{1,0:T(8,128)(2,1)S(1)} %collective-permute-done.13.refs_1_), channel_id=1, source_target_pairs={{0,2},{1,5},{2,0},{3,7},{4,6},{5,1},{6,4},{7,3},{8,10},{9,13},{10,... | collective-permute-start | bytes 1032200 | tf_op jit(solution)/shard_map/ppermute | solution.py:104
  40.0 6.6 %collective-permute-start.21 = (bf16[24,1152]{1,0:T(8,128)(2,1)S(1)}, bf16[24,1152]{1,0:T(8,128)(2,1)S(1)}, u32[]{:S(2)}, u32[]{:S(2)}) collective-permute-start(bf16[24,1152]{1,0:T(8,128)(2,1)S(1)} %copy-done.23), channel_id=1, source_target_pairs={{0,16},{1,17},{2,18},{3,19},{4,20},{5,21},{6,22},{7,23},{8,24},{9,... | collective-permute-start | bytes 165896 | tf_op jit(solution)/shard_map/ppermute | solution.py:104
  52.5 7.5 %collective-permute-start.7 = (bf16[96,1792]{1,0:T(8,128)(2,1)}, bf16[96,1792]{1,0:T(8,128)(2,1)S(1)}, u32[]{:S(2)}, u32[]{:S(2)}) collective-permute-start(bf16[96,1792]{1,0:T(8,128)(2,1)} %shard_map.291.refs_0_), channel_id=1, source_target_pairs={{0,2},{1,5},{2,0},{3,7},{4,6},{5,1},{6,4},{7,3},{8,10},{9,13},{10,... | collective-permute-start | bytes 1032200 | tf_op jit(solution)/shard_map/ppermute | solution.py:104
  54.4 6.1 %collective-permute-start.18 = (bf16[96,1792]{1,0:T(8,128)(2,1)S(1)}, bf16[96,1792]{1,0:T(8,128)(2,1)S(1)}, u32[]{:S(2)}, u32[]{:S(2)}) collective-permute-start(bf16[96,1792]{1,0:T(8,128)(2,1)S(1)} %collective-permute-done.14.refs_2_), channel_id=1, source_target_pairs={{0,1},{1,0},{2,3},{3,2},{4,5},{5,4},{6,7},{7,6},{8,9},{9,8},{10,11... | collective-permute-start | bytes 1032200 | tf_op jit(solution)/shard_map/ppermute | solution.py:107
  54.9 8.8 %collective-permute-start.8 = (bf16[96,1792]{1,0:T(8,128)(2,1)S(1)}, bf16[96,1792]{1,0:T(8,128)(2,1)S(1)}, u32[]{:S(2)}, u32[]{:S(2)}) collective-permute-start(bf16[96,1792]{1,0:T(8,128)(2,1)S(1)} %collective-permute-done.6.refs_1_), channel_id=1, source_target_pairs={{0,2},{1,5},{2,0},{3,7},{4,6},{5,1},{6,4},{7,3},{8,10},{9,13},{10,... | collective-permute-start | bytes 1032200 | tf_op jit(solution)/shard_map/ppermute | solution.py:104
  55.1 8.6 %collective-permute-start.19 = (bf16[96,1792]{1,0:T(8,128)(2,1)S(1)}, bf16[96,1792]{1,0:T(8,128)(2,1)S(1)}, u32[]{:S(2)}, u32[]{:S(2)}) collective-permute-start(bf16[96,1792]{1,0:T(8,128)(2,1)S(1)} %collective-permute-done.15.refs_3_), channel_id=1, source_target_pairs={{0,1},{1,0},{2,3},{3,2},{4,5},{5,4},{6,7},{7,6},{8,9},{9,8},{10,11... | collective-permute-start | bytes 1032200 | tf_op jit(solution)/shard_map/ppermute | solution.py:107
  60.0 17.6 %collective-permute-start.9 = (bf16[96,1792]{1,0:T(8,128)(2,1)S(1)}, bf16[96,1792]{1,0:T(8,128)(2,1)S(1)}, u32[]{:S(2)}, u32[]{:S(2)}) collective-permute-start(bf16[96,1792]{1,0:T(8,128)(2,1)S(1)} %copy-done.4), channel_id=1, source_target_pairs={{0,1},{1,0},{2,3},{3,2},{4,5},{5,4},{6,7},{7,6},{8,9},{9,8},{10,11... | collective-permute-start | bytes 1032200 | tf_op jit(solution)/shard_map/ppermute | solution.py:107
  60.0 17.6 %collective-permute-start.10 = (bf16[96,1792]{1,0:T(8,128)(2,1)S(1)}, bf16[96,1792]{1,0:T(8,128)(2,1)S(1)}, u32[]{:S(2)}, u32[]{:S(2)}) collective-permute-start(bf16[96,1792]{1,0:T(8,128)(2,1)S(1)} %collective-permute-done.6.refs_1_), channel_id=1, source_target_pairs={{0,1},{1,0},{2,3},{3,2},{4,5},{5,4},{6,7},{7,6},{8,9},{9,8},{10,11... | collective-permute-start | bytes 1032200 | tf_op jit(solution)/shard_map/ppermute | solution.py:107
  60.5 17.1 %collective-permute-start.11 = (bf16[96,1792]{1,0:T(8,128)(2,1)S(1)}, bf16[96,1792]{1,0:T(8,128)(2,1)S(1)}, u32[]{:S(2)}, u32[]{:S(2)}) collective-permute-start(bf16[96,1792]{1,0:T(8,128)(2,1)S(1)} %collective-permute-done.7.refs_2_), channel_id=1, source_target_pairs={{0,1},{1,0},{2,3},{3,2},{4,5},{5,4},{6,7},{7,6},{8,9},{9,8},{10,11... | collective-permute-start | bytes 1032200 | tf_op jit(solution)/shard_map/ppermute | solution.py:107
  63.7 13.9 %collective-permute-start.12 = (bf16[96,1792]{1,0:T(8,128)(2,1)S(1)}, bf16[96,1792]{1,0:T(8,128)(2,1)S(1)}, u32[]{:S(2)}, u32[]{:S(2)}) collective-permute-start(bf16[96,1792]{1,0:T(8,128)(2,1)S(1)} %collective-permute-done.8.refs_3_), channel_id=1, source_target_pairs={{0,1},{1,0},{2,3},{3,2},{4,5},{5,4},{6,7},{7,6},{8,9},{9,8},{10,11... | collective-permute-start | bytes 1032200 | tf_op jit(solution)/shard_map/ppermute | solution.py:107
  108.2 9.5 %collective-permute-start.23 = (bf16[96,1152]{1,0:T(8,128)(2,1)S(1)}, bf16[96,1152]{1,0:T(8,128)(2,1)S(1)}, u32[]{:S(2)}, u32[]{:S(2)}) collective-permute-start(bf16[96,1152]{1,0:T(8,128)(2,1)S(1)} %copy-done.6), channel_id=1, source_target_pairs={{0,4},{1,3},{2,6},{3,1},{4,0},{5,7},{6,2},{7,5},{8,12},{9,11},{10,... | collective-permute-start | bytes 663560 | tf_op jit(solution)/shard_map/ppermute | solution.py:104
  115.8 18.3 %collective-permute-start.26 = (bf16[192,1792]{1,0:T(8,128)(2,1)}, bf16[192,1792]{1,0:T(8,128)(2,1)S(1)}, u32[]{:S(2)}, u32[]{:S(2)}) collective-permute-start(bf16[192,1792]{1,0:T(8,128)(2,1)} %get-tuple-element.97), channel_id=1, source_target_pairs={{0,2},{1,5},{2,0},{3,7},{4,6},{5,1},{6,4},{7,3},{8,10},{9,13},{10,... | collective-permute-start | bytes 2064392 | tf_op jit(solution)/shard_map/ppermute | solution.py:104
  117.7 11.7 %collective-permute-start.24 = (bf16[96,1152]{1,0:T(8,128)(2,1)S(1)}, bf16[96,1152]{1,0:T(8,128)(2,1)S(1)}, u32[]{:S(2)}, u32[]{:S(2)}) collective-permute-start(bf16[96,1152]{1,0:T(8,128)(2,1)S(1)} %collective-permute-done.23.refs_9_), channel_id=1, source_target_pairs={{0,2},{1,5},{2,0},{3,7},{4,6},{5,1},{6,4},{7,3},{8,10},{9,13},{10,... | collective-permute-start | bytes 663560 | tf_op jit(solution)/shard_map/ppermute | solution.py:104
  137.5 13.0 %collective-permute-start.27 = (bf16[96,1792]{1,0:T(8,128)(2,1)}, bf16[96,1792]{1,0:T(8,128)(2,1)S(1)}, u32[]{:S(2)}, u32[]{:S(2)}) collective-permute-start(bf16[96,1792]{1,0:T(8,128)(2,1)} %get-tuple-element.101), channel_id=1, source_target_pairs={{0,4},{1,3},{2,6},{3,1},{4,0},{5,7},{6,2},{7,5},{8,12},{9,11},{10,... | collective-permute-start | bytes 1032200 | tf_op jit(solution)/shard_map/ppermute | solution.py:104
  162.4 32.3 %collective-permute-start.46 = (bf16[384,640]{1,0:T(8,128)(2,1)}, bf16[384,640]{1,0:T(8,128)(2,1)S(1)}, u32[]{:S(2)}, u32[]{:S(2)}) collective-permute-start(bf16[384,640]{1,0:T(8,128)(2,1)} %get-tuple-element.118), channel_id=1, source_target_pairs={{0,1},{1,0},{2,3},{3,2},{4,5},{5,4},{6,7},{7,6},{8,9},{9,8},{10,11... | collective-permute-start | bytes 1474568 | tf_op jit(solution)/shard_map/ppermute | solution.py:107
  162.6 10.0 %collective-permute-start.29 = (bf16[24,1792]{1,0:T(8,128)(2,1)S(1)}, bf16[24,1792]{1,0:T(8,128)(2,1)S(1)}, u32[]{:S(2)}, u32[]{:S(2)}) collective-permute-start(bf16[24,1792]{1,0:T(8,128)(2,1)S(1)} %copy-done.71), channel_id=1, source_target_pairs={{0,16},{1,17},{2,18},{3,19},{4,20},{5,21},{6,22},{7,23},{8,24},{9,... | collective-permute-start | bytes 258056 | tf_op jit(solution)/shard_map/ppermute | solution.py:104
  165.1 7.6 %collective-permute-start.30 = (bf16[24,1792]{1,0:T(8,128)(2,1)S(1)}, bf16[24,1792]{1,0:T(8,128)(2,1)S(1)}, u32[]{:S(2)}, u32[]{:S(2)}) collective-permute-start(bf16[24,1792]{1,0:T(8,128)(2,1)S(1)} %copy-done.70), channel_id=1, source_target_pairs={{0,24},{1,25},{2,26},{3,27},{4,28},{5,29},{6,30},{7,31},{8,16},{9,... | collective-permute-start | bytes 258056 | tf_op jit(solution)/shard_map/ppermute | solution.py:104
  177.1 11.2 %collective-permute-start.32 = (bf16[32,1792]{1,0:T(8,128)(2,1)}, bf16[32,1792]{1,0:T(8,128)(2,1)S(1)}, u32[]{:S(2)}, u32[]{:S(2)}) collective-permute-start(bf16[32,1792]{1,0:T(8,128)(2,1)} %get-tuple-element.115.refs_0_), channel_id=1, source_target_pairs={{0,16},{1,17},{2,18},{3,19},{4,20},{5,21},{6,22},{7,23},{8,24},{9,... | collective-permute-start | bytes 344072 | tf_op jit(solution)/shard_map/ppermute | solution.py:104
  177.8 10.5 %collective-permute-start.33 = (bf16[32,1792]{1,0:T(8,128)(2,1)}, bf16[32,1792]{1,0:T(8,128)(2,1)S(1)}, u32[]{:S(2)}, u32[]{:S(2)}) collective-permute-start(bf16[32,1792]{1,0:T(8,128)(2,1)} %get-tuple-element.115.refs_0_), channel_id=1, source_target_pairs={{0,24},{1,25},{2,26},{3,27},{4,28},{5,29},{6,30},{7,31},{8,16},{9,... | collective-permute-start | bytes 344072 | tf_op jit(solution)/shard_map/ppermute | solution.py:104
  191.5 31.6 %collective-permute-start.34 = (bf16[128,1792]{1,0:T(8,128)(2,1)}, bf16[128,1792]{1,0:T(8,128)(2,1)S(1)}, u32[]{:S(2)}, u32[]{:S(2)}) collective-permute-start(bf16[128,1792]{1,0:T(8,128)(2,1)} %shard_map.305.refs_0_), channel_id=1, source_target_pairs={{0,4},{1,3},{2,6},{3,1},{4,0},{5,7},{6,2},{7,5},{8,12},{9,11},{10,... | collective-permute-start | bytes 1376264 | tf_op jit(solution)/shard_map/ppermute | solution.py:104
  193.2 48.8 %collective-permute-start.35 = (bf16[128,1792]{1,0:T(8,128)(2,1)}, bf16[128,1792]{1,0:T(8,128)(2,1)S(1)}, u32[]{:S(2)}, u32[]{:S(2)}) collective-permute-start(bf16[128,1792]{1,0:T(8,128)(2,1)} %shard_map.305.refs_0_), channel_id=1, source_target_pairs={{0,2},{1,5},{2,0},{3,7},{4,6},{5,1},{6,4},{7,3},{8,10},{9,13},{10,... | collective-permute-start | bytes 1376264 | tf_op jit(solution)/shard_map/ppermute | solution.py:104
  197.7 10.1 %collective-permute-start.47 = (bf16[96,640]{1,0:T(8,128)(2,1)}, bf16[96,640]{1,0:T(8,128)(2,1)S(1)}, u32[]{:S(2)}, u32[]{:S(2)}) collective-permute-start(bf16[96,640]{1,0:T(8,128)(2,1)} %get-tuple-element.120), channel_id=1, source_target_pairs={{0,4},{1,3},{2,6},{3,1},{4,0},{5,7},{6,2},{7,5},{8,12},{9,11},{10,... | collective-permute-start | bytes 368648 | tf_op jit(solution)/shard_map/ppermute | solution.py:104
  198.2 9.6 %collective-permute-start.48 = (bf16[96,640]{1,0:T(8,128)(2,1)}, bf16[96,640]{1,0:T(8,128)(2,1)S(1)}, u32[]{:S(2)}, u32[]{:S(2)}) collective-permute-start(bf16[96,640]{1,0:T(8,128)(2,1)} %get-tuple-element.121), channel_id=1, source_target_pairs={{0,2},{1,5},{2,0},{3,7},{4,6},{5,1},{6,4},{7,3},{8,10},{9,13},{10,... | collective-permute-start | bytes 368648 | tf_op jit(solution)/shard_map/ppermute | solution.py:104
  198.5 9.3 %collective-permute-start.49 = (bf16[96,640]{1,0:T(8,128)(2,1)}, bf16[96,640]{1,0:T(8,128)(2,1)S(1)}, u32[]{:S(2)}, u32[]{:S(2)}) collective-permute-start(bf16[96,640]{1,0:T(8,128)(2,1)} %get-tuple-element.122), channel_id=1, source_target_pairs={{0,6},{1,7},{2,4},{3,5},{4,2},{5,3},{6,0},{7,1},{8,14},{9,15},{10,... | collective-permute-start | bytes 368648 | tf_op jit(solution)/shard_map/ppermute | solution.py:104
  223.0 20.4 %collective-permute-start.37 = (bf16[128,1792]{1,0:T(8,128)(2,1)S(1)}, bf16[128,1792]{1,0:T(8,128)(2,1)S(1)}, u32[]{:S(2)}, u32[]{:S(2)}) collective-permute-start(bf16[128,1792]{1,0:T(8,128)(2,1)S(1)} %copy-done.3), channel_id=1, source_target_pairs={{0,1},{1,0},{2,3},{3,2},{4,5},{5,4},{6,7},{7,6},{8,9},{9,8},{10,11... | collective-permute-start | bytes 1376264 | tf_op jit(solution)/shard_map/ppermute | solution.py:107
  223.1 25.1 %collective-permute-start.36 = (bf16[128,1792]{1,0:T(8,128)(2,1)S(1)}, bf16[128,1792]{1,0:T(8,128)(2,1)S(1)}, u32[]{:S(2)}, u32[]{:S(2)}) collective-permute-start(bf16[128,1792]{1,0:T(8,128)(2,1)S(1)} %collective-permute-done.34.refs_1_), channel_id=1, source_target_pairs={{0,2},{1,5},{2,0},{3,7},{4,6},{5,1},{6,4},{7,3},{8,10},{9,13},{10,... | collective-permute-start | bytes 1376264 | tf_op jit(solution)/shard_map/ppermute | solution.py:104
  223.8 17.2 %collective-permute-start.41 = (bf16[96,1152]{1,0:T(8,128)(2,1)S(1)}, bf16[96,1152]{1,0:T(8,128)(2,1)S(1)}, u32[]{:S(2)}, u32[]{:S(2)}) collective-permute-start(bf16[96,1152]{1,0:T(8,128)(2,1)S(1)} %copy-done.6), channel_id=1, source_target_pairs={{0,2},{1,5},{2,0},{3,7},{4,6},{5,1},{6,4},{7,3},{8,10},{9,13},{10,... | collective-permute-start | bytes 663560 | tf_op jit(solution)/shard_map/ppermute | solution.py:104
  242.0 6.1 %collective-permute-start.59 = (bf16[96,640]{1,0:T(8,128)(2,1)}, bf16[96,640]{1,0:T(8,128)(2,1)}, u32[]{:S(2)}, u32[]{:S(2)}) collective-permute-start(bf16[96,640]{1,0:T(8,128)(2,1)} %shard_map.310.refs_8_), channel_id=1, source_target_pairs={{0,6},{1,7},{2,4},{3,5},{4,2},{5,3},{6,0},{7,1},{8,14},{9,15},{10,... | collective-permute-start | bytes 368648 | tf_op jit(solution)/shard_map/ppermute | solution.py:104
  243.5 14.3 %collective-permute-start.38 = (bf16[128,1792]{1,0:T(8,128)(2,1)S(1)}, bf16[128,1792]{1,0:T(8,128)(2,1)S(1)}, u32[]{:S(2)}, u32[]{:S(2)}) collective-permute-start(bf16[128,1792]{1,0:T(8,128)(2,1)S(1)} %collective-permute-done.34.refs_1_), channel_id=1, source_target_pairs={{0,1},{1,0},{2,3},{3,2},{4,5},{5,4},{6,7},{7,6},{8,9},{9,8},{10,11... | collective-permute-start | bytes 1376264 | tf_op jit(solution)/shard_map/ppermute | solution.py:107
  245.0 12.9 %collective-permute-start.39 = (bf16[128,1792]{1,0:T(8,128)(2,1)S(1)}, bf16[128,1792]{1,0:T(8,128)(2,1)S(1)}, u32[]{:S(2)}, u32[]{:S(2)}) collective-permute-start(bf16[128,1792]{1,0:T(8,128)(2,1)S(1)} %collective-permute-done.35.refs_2_), channel_id=1, source_target_pairs={{0,1},{1,0},{2,3},{3,2},{4,5},{5,4},{6,7},{7,6},{8,9},{9,8},{10,11... | collective-permute-start | bytes 1376264 | tf_op jit(solution)/shard_map/ppermute | solution.py:107
  248.1 10.2 %collective-permute-start.40 = (bf16[128,1792]{1,0:T(8,128)(2,1)S(1)}, bf16[128,1792]{1,0:T(8,128)(2,1)S(1)}, u32[]{:S(2)}, u32[]{:S(2)}) collective-permute-start(bf16[128,1792]{1,0:T(8,128)(2,1)S(1)} %collective-permute-done.36.refs_3_), channel_id=1, source_target_pairs={{0,1},{1,0},{2,3},{3,2},{4,5},{5,4},{6,7},{7,6},{8,9},{9,8},{10,11... | collective-permute-start | bytes 1376264 | tf_op jit(solution)/shard_map/ppermute | solution.py:107
  249.5 7.8 %collective-permute-start.62 = (bf16[96,640]{1,0:T(8,128)(2,1)}, bf16[96,640]{1,0:T(8,128)(2,1)}, u32[]{:S(2)}, u32[]{:S(2)}) collective-permute-start(bf16[96,640]{1,0:T(8,128)(2,1)} %collective-permute-done.58.refs_10_), channel_id=1, source_target_pairs={{0,1},{1,0},{2,3},{3,2},{4,5},{5,4},{6,7},{7,6},{8,9},{9,8},{10,11... | collective-permute-start | bytes 368648 | tf_op jit(solution)/shard_map/ppermute | solution.py:107
  250.1 7.2 %collective-permute-start.63 = (bf16[96,640]{1,0:T(8,128)(2,1)}, bf16[96,640]{1,0:T(8,128)(2,1)}, u32[]{:S(2)}, u32[]{:S(2)}) collective-permute-start(bf16[96,640]{1,0:T(8,128)(2,1)} %collective-permute-done.59.refs_11_), channel_id=1, source_target_pairs={{0,1},{1,0},{2,3},{3,2},{4,5},{5,4},{6,7},{7,6},{8,9},{9,8},{10,11... | collective-permute-start | bytes 368648 | tf_op jit(solution)/shard_map/ppermute | solution.py:107
  257.3 9.9 %collective-permute-start.42 = (bf16[96,1152]{1,0:T(8,128)(2,1)S(1)}, bf16[96,1152]{1,0:T(8,128)(2,1)S(1)}, u32[]{:S(2)}, u32[]{:S(2)}) collective-permute-start(bf16[96,1152]{1,0:T(8,128)(2,1)S(1)} %copy-done.6), channel_id=1, source_target_pairs={{0,1},{1,0},{2,3},{3,2},{4,5},{5,4},{6,7},{7,6},{8,9},{9,8},{10,11... | collective-permute-start | bytes 663560 | tf_op jit(solution)/shard_map/ppermute | solution.py:107
  257.4 9.8 %collective-permute-start.43 = (bf16[96,1152]{1,0:T(8,128)(2,1)}, bf16[96,1152]{1,0:T(8,128)(2,1)S(1)}, u32[]{:S(2)}, u32[]{:S(2)}) collective-permute-start(bf16[96,1152]{1,0:T(8,128)(2,1)} %copy-done.60), channel_id=1, source_target_pairs={{0,1},{1,0},{2,3},{3,2},{4,5},{5,4},{6,7},{7,6},{8,9},{9,8},{10,11... | collective-permute-start | bytes 663560 | tf_op jit(solution)/shard_map/ppermute | solution.py:107
  257.8 9.4 %collective-permute-start.44 = (bf16[96,1152]{1,0:T(8,128)(2,1)}, bf16[96,1152]{1,0:T(8,128)(2,1)S(1)}, u32[]{:S(2)}, u32[]{:S(2)}) collective-permute-start(bf16[96,1152]{1,0:T(8,128)(2,1)} %copy-done.62), channel_id=1, source_target_pairs={{0,1},{1,0},{2,3},{3,2},{4,5},{5,4},{6,7},{7,6},{8,9},{9,8},{10,11... | collective-permute-start | bytes 663560 | tf_op jit(solution)/shard_map/ppermute | solution.py:107
  257.9 9.4 %collective-permute-start.45 = (bf16[96,1152]{1,0:T(8,128)(2,1)}, bf16[96,1152]{1,0:T(8,128)(2,1)S(1)}, u32[]{:S(2)}, u32[]{:S(2)}) collective-permute-start(bf16[96,1152]{1,0:T(8,128)(2,1)} %copy-done.61), channel_id=1, source_target_pairs={{0,1},{1,0},{2,3},{3,2},{4,5},{5,4},{6,7},{7,6},{8,9},{9,8},{10,11... | collective-permute-start | bytes 663560 | tf_op jit(solution)/shard_map/ppermute | solution.py:107
  267.2 16.8 %collective-permute-start.64 = (bf16[24,640]{1,0:T(8,128)(2,1)}, bf16[24,640]{1,0:T(8,128)(2,1)S(1)}, u32[]{:S(2)}, u32[]{:S(2)}) collective-permute-start(bf16[24,640]{1,0:T(8,128)(2,1)} %get-tuple-element.135), channel_id=1, source_target_pairs={{0,1},{1,0},{2,3},{3,2},{4,5},{5,4},{6,7},{7,6},{8,9},{9,8},{10,11... | collective-permute-start | bytes 92168 | tf_op jit(solution)/shard_map/ppermute | solution.py:107
  (91 other events, 688.8 us)
where the time goes:
time: 290 us; the launch traced here: 287 us
  Pallas kernels  122 us (42%)
  waiting for transfers between devices  76.6 us (26%)
  starting transfers between devices  61.2 us (21%)
  local copies, waits for them, and re-layouts  19.6 us (7%)
  other arithmetic  6.29 us (2%)
    ppermute x41, waiting for transfers between devices, swap(): return lax.ppermute(value, AXES, pairs)  74.5 us
    ppermute x41, starting transfers between devices, swap(): return lax.ppermute(value, AXES, pairs)  55.2 us
    pallas_call x15, Pallas kernels, fused(): pl.pallas_call(kernel, out_shape=[struct(member.shape, member.dtype) for...  29.3 us
    pallas_call x1, Pallas kernels, run_hidden(): pl.pallas_call(hidden_kernel, grid=(samples,), in_specs=[SMEM_WHOLE, SMEM...  29 us
    pallas_call x4, Pallas kernels, run_whole(): pl.pallas_call(kernel, in_specs=[SMEM_WHOLE] + [vmem] * len(operands), ou...  28.7 us
    pallas_call x3, Pallas kernels, run_scores(): pl.pallas_call(scores_kernel, grid=(count,), in_specs=[each(member.shape,...  16.8 us
    unnamed x149, local copies, waits for them, and re-layouts  15.6 us
    pallas_call x1, Pallas kernels, run_closing(): pl.pallas_call(functools.partial(closing_kernel, starts), grid=(samples,)...  9.21 us
  transfers between devices with their start and end apart: 65, of which 23 were waited for; matrix products, arithmetic and copies ran while one was open for 3% of the time, Pallas kernels for 26%

commit v1 on v0

--- a/solution.py
+++ b/solution.py
@@ -109,19 +109,21 @@
     def far(self, value, stride, step):
         return self.swap(value, (4 * stride * step, 4 * stride * step))
 
-    def gather_far(self, block, rows):
+    def join(self, pieces, rows):
+        def body(*pieces):
+            wide = [piece.astype(F32) for piece in pieces]
+            parts = [piece[:rows] for piece in wide]
+            if rows < wide[0].shape[0]:
+                parts = parts + [piece[rows:] for piece in wide]
+            return jnp.concatenate(parts, axis=0).astype(BF16)
+
+        return fused(body, *pieces, plain=rows % 8 > 0)
+
+    def gather_far(self, block, rows, skip=0):
         held = block
-        for stride, radix in self.digits:
+        for stride, radix in self.digits[skip:]:
             arrived = [self.far(held, stride, step) for step in range(1, radix)]
-
-            def join(*pieces, rows=rows):
-                wide = [piece.astype(F32) for piece in pieces]
-                parts = [piece[:rows] for piece in wide]
-                if rows < wide[0].shape[0]:
-                    parts = parts + [piece[rows:] for piece in wide]
-                return jnp.concatenate(parts, axis=0).astype(BF16)
-
-            held = fused(join, held, *arrived, plain=rows % 8 > 0)
+            held = self.join([held] + arrived, rows)
             rows = rows * radix
         return held
 
@@ -310,8 +312,8 @@
 def hidden_kernel(place_ref, counts_ref, *refs):
     own_refs, other_refs = refs[:4], refs[4:8]
     x_ref, cot_ref, mixed_ref, modes_ref, bias_ref, order_ref = refs[8:14]
-    out_ref, dmix_ref, dx_ref, dmodes_ref, dbias_ref, mine_ref, give_ref = refs[14:21]
-    total_ref, fc1_ref, fc2_ref, wproj_ref = refs[21:]
+    out_ref, dmix_ref, dx_ref, dmodes_ref, dbias_ref, mine_ref, give_ref, moment_ref = refs[14:22]
+    total_ref, fc1_ref, fc2_ref, wproj_ref = refs[22:]
     step = pl.program_id(0)
     core = place_ref[0]
     features = x_ref.shape[-1]
@@ -327,12 +329,17 @@
         halves = halves_of(core, own_refs, other_refs)
         for side in range(2):
             order = order_ref[:, side * features : (side + 1) * features]
-            sorted_half = dot(order, halves[side]).astype(BF16)
+            sorted_half = dot(order, halves[side][:, : mine_ref.shape[1]]).astype(BF16)
             fc1_ref[:, side * half : (side + 1) * half] = sorted_half[:, :half]
             fc2_ref[:, side * half : (side + 1) * half] = sorted_half[:, half:hidden]
             wproj_ref[:, side * small : (side + 1) * small] = sorted_half[
                 :, hidden : hidden + small
             ]
+        quarter = features // 4
+        for index, place in enumerate((0, 2, 1, 3)):
+            window = slice(index * quarter, (index + 1) * quarter)
+            moment_ref[0, window] = own_refs[index][:, mine_ref.shape[1] :]
+            moment_ref[1, window] = other_refs[place][:, mine_ref.shape[1] :]
 
     def mode(index):
         return modes_ref[0, :, index * features : (index + 1) * features]
@@ -447,7 +454,8 @@
 def closing_kernel(starts, place_ref, *refs):
     parts, refs = refs[: len(starts)], refs[len(starts) :]
     x_ref, dx_ref, modes_ref, attn_in_ref, first_ref, wqkv_ref, order_ref = refs[:7]
-    grad_ref, dmodes_ref, dbias_ref, mine_ref, give_ref, total_ref = refs[7:]
+    act_ref, rest_bias_ref = refs[7:9]
+    grad_ref, dmodes_ref, message_ref, mine_ref, give_ref, total_ref, dbias_ref, rows_ref = refs[9:]
     step = pl.program_id(0)
     features = x_ref.shape[-1]
     middle = features // 2
@@ -472,13 +480,39 @@
     normed, spread = layer_stats(x_ref[0].astype(F32))
     scaling = modes_ref[0, :, features : 2 * features]
     grad_ref[0] = dx_ref[0] + layer_back(normed, spread, grad_attn_in * (1.0 + scaling))
-    dmodes_ref[0, :, :features] = column_sum(grad_attn_in).astype(BF16)
-    dmodes_ref[0, :, features : 2 * features] = column_sum(grad_attn_in * normed).astype(BF16)
-    dmodes_ref[0, :, 2 * features :] = first_ref[0, :, 2 * features :].astype(BF16)
+    row = jnp.concatenate(
+        [
+            column_sum(grad_attn_in),
+            column_sum(grad_attn_in * normed),
+            first_ref[0, :, 2 * features :],
+        ],
+        axis=1,
+    )
+    rows_ref[step] = row
+    dmodes_ref[0] = row.astype(BF16)
 
     @pl.when(step == pl.num_programs(0) - 1)
     def _():
         core = place_ref[0]
+        samples, wide = rows_ref.shape[0], message_ref.shape[1]
+        bias = jnp.concatenate([dbias_ref[...], rest_bias_ref[...]], axis=1)
+        share = bias.shape[1] // samples
+        row = lax.broadcasted_iota(jnp.int32, message_ref.shape, 0)
+        message = jnp.zeros(message_ref.shape, F32)
+        for index in range(samples):
+            grad = rows_ref[index]
+            late = jnp.concatenate(
+                [
+                    grad[:, wide:],
+                    act_ref[index : index + 1, :].astype(F32),
+                    bias[:, index * share : (index + 1) * share],
+                    jnp.zeros((1, 2 * wide - 7 * features - share), F32),
+                ],
+                axis=1,
+            )
+            message = jnp.where(row == index, grad[:, :wide], message)
+            message = jnp.where(row == samples + index, late, message)
+        message_ref[...] = message.astype(BF16)
         mine_ref[...] = total_ref[core]
         give_ref[...] = total_ref[1 - core].astype(BF16)
 
@@ -491,40 +525,27 @@
         gram = sum(dot_columns(part, part) for part in current).astype(BF16)
         poly = (coef_two * gram.astype(F32) + coef_three * dot(gram, gram)).astype(BF16)
         if iteration == ITERS - 1:
-            poly = poly[:rows]
-            return [
-                (coef_one * part[:rows].astype(F32) + dot(poly, part)).astype(BF16)
-                for part in current
-            ]
+            part = current[0]
+            return coef_one * part[:rows].astype(F32) + dot(poly[:rows], part)
         current = [
             (coef_one * part.astype(F32) + dot(poly, part)).astype(BF16) for part in current
         ]
 
 
-def stacked_parts(own, other, extent, window):
-    return [
-        jnp.concatenate([group[i][:extent, window] for i in order], axis=0).astype(F32)
-        for group, order in ((own, (0, 1, 2, 3)), (other, (0, 2, 1, 3)))
-    ]
-
-
-def first_muon_kernel(place_ref, *refs):
-    groups = [refs[4 * index : 4 * index + 4] for index in range(4)]
-    moment_ref, orders_ref, early_ref, late_ref, sums_ref = refs[16:21]
-    keep_ref, give_ref, new_moment_ref, bias_ref = refs[21:]
-    core = place_ref[0]
+def message_kernel(place_ref, *refs):
+    moment_ref, orders_ref, early_ref, late_ref, sums_ref = refs[8:13]
+    new_moment_ref, bias_ref, modes_ref, act_ref = refs[13:]
     features = orders_ref.shape[0]
-    rows = moment_ref.shape[0]
-    quarter = features // 4
-    wide = groups[0][0].shape[1]
-    half = moment_ref.shape[1]
-
-    messages = jnp.concatenate([ref[quarter:, :] for ref in groups[0] + groups[1]], axis=0)
+    rows, half = moment_ref.shape
+    messages = jnp.concatenate([ref[...] for ref in refs[:8]], axis=0)
     early = dot(early_ref[...], messages).astype(BF16)
     late = dot(late_ref[...], messages).astype(BF16)
-    rest = 6 * features - wide
+    rest = 6 * features - early.shape[1]
     modes = jnp.concatenate([early, late[:, :rest]], axis=1)
-    act = dot(late[:, rest : rest + features], orders_ref[:, :features]).astype(BF16)
+    modes_ref[...] = modes
+    both = dot(late[:, rest : rest + features], orders_ref[...]).astype(BF16)
+    act = jnp.where(place_ref[0] == 0, both[:, :features], both[:, features:])
+    act_ref[...] = act
     sums = dot(sums_ref[...], late[:, rest + features :])
     bias_ref[:, : 6 * features] = column_sum(modes.astype(F32))
     samples = sums_ref.shape[0] - 4
@@ -532,60 +553,68 @@
     for index in range(samples):
         start = 6 * features + index * extent
         bias_ref[:, start : start + extent] = sums[index : index + 1, :extent]
-    modes_here = jnp.where(core == 0, modes[:, :half], modes[:, half:])
+    modes_here = jnp.where(place_ref[0] == 0, modes[:, :half], modes[:, half:])
     part = dot_rows(act[:, :rows], modes_here)
     new_moment_ref[...] = momentum_decay * moment_ref[...] + part
 
-    keep_ref[...] = jnp.zeros_like(keep_ref)
-    give_ref[...] = jnp.zeros_like(give_ref)
-
-    @pl.when(core == 0)
+
+def muon_kernel(rows, place_ref, *refs):
+    own_refs, other_refs = refs[:4], refs[4:8]
+    moment_ref, modes_ref, act_ref = refs[8:11]
+    result_refs = refs[11:]
+    core, role = place_ref[0], place_ref[2]
+    half = moment_ref.shape[2]
+    narrow = own_refs[0].shape[1]
+    split = narrow * 3 // 4
+
+    def stacked():
+        return [
+            jnp.concatenate([group[index][...] for index in order], axis=0).astype(F32)
+            for group, order in ((own_refs, (0, 1, 2, 3)), (other_refs, (0, 2, 1, 3)))
+        ]
+
+    def store(result, window):
+        for index, ref in enumerate(result_refs):
+            ref[:, window] = result[index * rows : (index + 1) * rows].astype(BF16)
+
+    @pl.when(role == 0)
     def _():
         grown = 1.0 + momentum_decay
-        moments = stacked_parts(groups[2], groups[3], quarter, slice(0, half))
+        sides = [modes_ref[:, :half], modes_ref[:, half:]]
+        ordered = [
+            jnp.where(core == 0, sides[0], sides[1]),
+            jnp.where(core == 0, sides[1], sides[0]),
+        ]
         update = [
-            grown * dot_rows(act, modes[:, side * half : (side + 1) * half])
-            + momentum_decay**2 * moments[side]
+            grown * dot_rows(act_ref[...], ordered[side])
+            + momentum_decay**2 * moment_ref[side].astype(F32)
             for side in range(2)
         ]
-        keep, give = orthogonal_rows(update, rows)
-        keep_ref[:, :half] = keep
-        give_ref[:, :half] = give
-
-    @pl.when(core == 1)
+        store(orthogonal_rows(update, 4 * rows), slice(0, half))
+
+    @pl.when(role != 0)
     def _():
-        for member in range(2):
-            window = slice(2 * member * features, 2 * (member + 1) * features)
-            parts = stacked_parts(groups[0], groups[1], quarter, window)
-            keep, give = orthogonal_rows(parts, rows)
-            keep_ref[:, window] = keep
-            give_ref[:, window] = give
-
-
-def second_muon_kernel(place_ref, *refs):
-    groups = [refs[4 * index : 4 * index + 4] for index in range(4)]
-    keep_ref, give_ref = refs[16:]
-    core = place_ref[0]
-    rows = keep_ref.shape[0]
-    quarter = groups[2][0].shape[0]
-    wide = groups[0][0].shape[1]
-    proj = wide - 16 * quarter
-    keep_ref[...] = jnp.zeros_like(keep_ref)
-    give_ref[...] = jnp.zeros_like(give_ref)
-
-    @pl.when(core == 0)
+        for ref in result_refs:
+            ref[...] = jnp.zeros_like(ref)
+
+    @pl.when((role == 1) | (role == 2))
     def _():
-        parts = stacked_parts(groups[2], groups[3], quarter, slice(0, keep_ref.shape[1]))
-        keep, give = orthogonal_rows(parts, rows)
-        keep_ref[...] = keep
-        give_ref[...] = give
-
-    @pl.when(core == 1)
+        store(orthogonal_rows(stacked(), 4 * rows), slice(0, narrow))
+
+    @pl.when(role == 3)
     def _():
-        parts = stacked_parts(groups[0], groups[1], quarter, slice(wide - proj, wide))
-        keep, give = orthogonal_rows(parts, rows)
-        keep_ref[:, :proj] = keep
-        give_ref[:, :proj] = give
+        parts = stacked()
+        lane = lax.broadcasted_iota(jnp.int32, parts[0].shape, 1)
+        low = split // 128 * 128
+        high = (split + 127) // 128 * 128
+        first = [jnp.where(lane < split, part, 0.0)[:, :high] for part in parts]
+        second = [jnp.where(lane >= split, part, 0.0)[:, low:] for part in parts]
+        first = orthogonal_rows(first, 4 * rows)
+        second = orthogonal_rows(second, 4 * rows)
+        store(first, slice(0, high))
+        first = jnp.where(lane[: 4 * rows, low:high] < split, first[:, low:], second[:, : high - low])
+        store(first, slice(low, high))
+        store(second[:, high - low :], slice(high, narrow))
 
 
 def whole(shape):
@@ -637,8 +666,8 @@
 
 def run_hidden(place, counts, own, other, x, cot, mixed, modes, bias, orders):
     samples, length, features = x.shape
-    wide = own[0].shape[1]
     hidden = 4 * features
+    wide = own[0].shape[1] - 3 * features
     results = [
         struct((samples, length, features), BF16),
         struct((samples, length, features), BF16),
@@ -647,6 +676,7 @@
         struct((1, 2 * features + hidden), F32),
         struct((features, wide), F32),
         struct((features, wide), BF16),
+        struct((2, features, 3 * features), BF16),
     ]
     return pl.pallas_call(
         hidden_kernel,
@@ -683,13 +713,13 @@
     )(qkv, lse, dmix)
 
 
-def run_closing(place, starts, parts, operands, wqkv, orders):
+def run_closing(place, starts, parts, operands, wqkv, orders, act, rest_bias, wide):
     samples, length, features = operands[0].shape
     padded = (3 * features // 2 + 127) // 128 * 128
     results = [
         struct((samples, length, features), F32),
         struct((samples, 1, 6 * features), BF16),
-        struct((1, 2 * features), F32),
+        struct((2 * samples, wide), BF16),
         struct((features, padded), F32),
         struct((features, padded), BF16),
     ]
@@ -706,14 +736,18 @@
         in_specs=[SMEM_WHOLE]
         + [part_spec(start, part) for start, part in zip(starts, parts)]
         + [each(member.shape) for member in operands]
-        + [whole(wqkv.shape), whole(orders.shape)],
+        + [whole(member.shape) for member in (wqkv, orders, act, rest_bias)],
         out_specs=[each(member.shape) for member in results[:2]]
         + [whole(member.shape) for member in results[2:]],
         out_shape=results,
-        scratch_shapes=[pltpu.VMEM((2, features, padded), F32)],
+        scratch_shapes=[
+            pltpu.VMEM((2, features, padded), F32),
+            pltpu.VMEM((1, 2 * features), F32),
+            pltpu.VMEM((samples, 1, 6 * features), F32),
+        ],
         compiler_params=params(),
         cost_estimate=cost(samples * length * features * 20000),
-    )(place, *parts, *operands, wqkv, orders)
+    )(place, *parts, *operands, wqkv, orders, act, rest_bias)
 
 
 def local(
@@ -750,7 +784,8 @@
     def tie(value, other):
         return lax.optimization_barrier((value, other))[0]
 
-    place = jnp.stack([core, links.me]).astype(jnp.int32)
+    role = links.me // 4 % 4
+    place = jnp.stack([core, links.me, role]).astype(jnp.int32)
 
     bias_here = biases.shape[0]
     bias_columns = bias_here // rows
@@ -762,18 +797,21 @@
         return jnp.concatenate(list(pieces) + [empty], axis=1).astype(BF16)
 
     block_first = fused(pack, w_ada, w_qkv, biases.reshape(rows, bias_columns), plain=plain)
-    block_rest, block_moment = fused(
-        lambda fc1, fc2, proj, moment: (pack(fc1, fc2, proj), moment.astype(BF16)),
+    first_held = links.gather_far(block_first, rows)
+    first_own = links.gather_near(first_held)
+    first_other = links.swap_pairs(first_own)
+    block_rest = fused(
+        lambda fc1, fc2, proj, moment, held: jnp.concatenate(
+            [pack(fc1, fc2, proj), moment.astype(BF16)], axis=1
+        ),
         w_fc1,
         w_fc2.T,
         w_proj,
         m_ada,
+        first_held[:16],
         plain=plain,
     )
-    first_held = links.gather_far(block_first, rows)
-    first_own = links.gather_near(first_held)
-    first_other = links.swap_pairs(first_own)
-    rest_held = links.gather_far(tie(block_rest, first_held), rows)
+    rest_held = links.gather_far(block_rest, rows)
     rest_own = links.gather_near(rest_held)
     rest_other = links.swap_pairs(rest_own)
 
@@ -802,19 +840,21 @@
 
     x = latents.reshape(samples, length, features)
     cot = cotangent.reshape(samples, length, features)
-    block_moment = tie(block_moment, rest_held)
     attn_in, qkv, log_totals, mixed = run_mix(x, modes, bias_all, qkv_full)
-    moment_held = links.gather_far(block_moment, rows)
-    mixed = tie(mixed, moment_held)
-    block_out, grad_mixed, grad_after, first_modes, bias_rest_sum, mine_rest, give_rest = run_hidden(
-        place, counts, rest_own, rest_other, x, cot, mixed, modes, bias_all, orders
-    )
-    moment_own = links.gather_near(moment_held)
+    (
+        block_out,
+        grad_mixed,
+        grad_after,
+        first_modes,
+        bias_rest_sum,
+        mine_rest,
+        give_rest,
+        moment_both,
+    ) = run_hidden(place, counts, rest_own, rest_other, x, cot, mixed, modes, bias_all, orders)
     rest_steps = links.scatter(mine_rest, give_rest, False)
     starts = (0, 1, samples - 1)
     counts_here = (1, samples - 2, 1)
     parts = []
-    grad_mixed = tie(grad_mixed, moment_own[3])
     kept_rest, arrived_rest = None, None
     for start, count in zip(starts, counts_here):
         part = run_scores(start, count, qkv, log_totals, grad_mixed)
@@ -822,14 +862,16 @@
         kept_rest, arrived_rest = next(rest_steps)
         grad_mixed, kept_rest = lax.optimization_barrier((grad_mixed, kept_rest))
     grad_after = tie(grad_after, kept_rest)
-    moment_other = links.swap_pairs(moment_own)
-    grad_latent, grad_modes, bias_qkv_sum, mine_qkv, give_qkv = run_closing(
+    grad_latent, grad_modes, message, mine_qkv, give_qkv = run_closing(
         place,
         starts,
         parts,
         [x, grad_after, modes, attn_in, first_modes],
         qkv_full,
         orders,
+        cond_act,
+        bias_rest_sum,
+        wide,
     )
     for kept_rest, arrived_rest in rest_steps:
         pass
@@ -842,72 +884,58 @@
         new_moment = momentum_decay * moment + kept
         return new_moment, kept + momentum_decay * new_moment
 
-    later = 6 * features - wide
-
-    def update_rest(kept, one, two, three, fc1, fc2, proj, grads, act, bias_qkv, bias_rest):
-        empty = jnp.zeros((rows, padded_proj), F32)
-        moment = jnp.concatenate([fc1, fc2, proj, empty], axis=1)
-        new_moment, direction = stepped(kept, [one, two, three], moment)
-        bias_flat = jnp.concatenate([bias_qkv, bias_rest], axis=1)
-        share = bias_flat.shape[1] // samples
-        row = lax.broadcasted_iota(jnp.int32, (2 * samples, wide), 0)
-        message = jnp.zeros((2 * samples, wide), F32)
-        for index in range(samples):
-            grad = grads[index].astype(F32)
-            late = jnp.concatenate(
-                [
-                    grad[:, wide:],
-                    act[index : index + 1].astype(F32),
-                    bias_flat[:, index * share : (index + 1) * share],
-                    jnp.zeros((1, wide - later - features - share), F32),
-                ],
-                axis=1,
-            )
-            message = jnp.where(row == index, grad[:, :wide], message)
-            message = jnp.where(row == samples + index, late, message)
-        block = jnp.concatenate([direction, message], axis=0).astype(BF16)
-        return (
-            new_moment[:, :half_fc],
-            new_moment[:, half_fc:hidden],
-            new_moment[:, hidden : hidden + half_proj],
-            block,
-        )
-
     def total_of(arrived):
         while len(arrived) < 3:
             arrived = arrived + [jnp.zeros_like(arrived[0])]
         return arrived
 
-    new_fc1, new_fc2, new_proj, update_block = fused(
-        update_rest,
+    message_own = links.gather_near(links.gather_far(message, 2 * samples))
+    message_other = links.swap_pairs(message_own)
+
+    def make_updates(role, *operands):
+        kept_rest, rest, kept_qkv, qkv = operands[0], operands[1:4], operands[4], operands[5:8]
+        m_fc1, m_fc2, m_proj, m_qkv = operands[8:]
+        moment = jnp.concatenate([m_fc1, m_fc2, m_proj, jnp.zeros((rows, padded_proj), F32)], axis=1)
+        new_rest, direction = stepped(kept_rest, rest, moment)
+        moment = jnp.concatenate([m_qkv, jnp.zeros((rows, padded_qkv), F32)], axis=1)
+        new_qkv, direction_qkv = stepped(kept_qkv, qkv, moment)
+        small = jnp.concatenate(
+            [direction_qkv[:, :half_qkv], direction[:, hidden : hidden + half_proj]], axis=1
+        )
+        choices = [direction[:, :half_fc], direction[:, half_fc:hidden], small]
+        blocks = []
+        for step in range(4):
+            target = role ^ step
+            chosen = jnp.where(target == 2, choices[1], choices[0])
+            blocks.append(jnp.where(target == 3, choices[2], chosen).astype(BF16))
+        return (
+            new_rest[:, :half_fc],
+            new_rest[:, half_fc:hidden],
+            new_rest[:, hidden : hidden + half_proj],
+            new_qkv[:, :half_qkv],
+            blocks,
+        )
+
+    role_array = jnp.broadcast_to(role.astype(jnp.int32), (1, 1))
+    new_fc1, new_fc2, new_proj, new_qkv, blocks = fused(
+        make_updates,
+        role_array,
         kept_rest,
         *total_of(arrived_rest),
+        kept_qkv,
+        *total_of(arrived_qkv),
         m_fc1,
         m_fc2.T,
         m_proj,
-        grad_modes,
-        cond_act,
-        bias_qkv_sum,
-        bias_rest_sum,
-        plain=plain,
-    )
-    update_own = links.gather_near(links.gather_far(update_block, rows))
-    update_other = links.swap_pairs(update_own)
-
-    def update_qkv(kept, one, two, three, moment):
-        moment = jnp.concatenate([moment, jnp.zeros((rows, padded_qkv), F32)], axis=1)
-        new_moment, direction = stepped(kept, [one, two, three], moment)
-        return new_moment[:, :half_qkv], direction.astype(BF16)
-
-    new_qkv, qkv_block = fused(
-        update_qkv,
-        kept_qkv,
-        *total_of(arrived_qkv),
         m_qkv,
         plain=plain,
     )
-    qkv_own = links.gather_direct(links.gather_far(qkv_block, rows))
-    qkv_other = links.swap_pairs(qkv_own)
+    stride, radix = links.digits[0]
+    update_held = links.join(
+        blocks[:1] + [links.far(blocks[step], stride, step) for step in range(1, radix)], rows
+    )
+    update_own = links.gather_near(links.gather_far(update_held, radix * rows, skip=1))
+    update_other = links.swap_pairs(update_own)
     grad_conditions = run_whole(
         condition_kernel,
         place,
@@ -915,7 +943,6 @@
         struct((samples, features), F32),
         10**9,
     )
-
     message_rows = 2 * samples * devices
     row = lax.broadcasted_iota(jnp.int32, (samples * devices, message_rows), 0)
     column = lax.broadcasted_iota(jnp.int32, (samples * devices, message_rows), 1)
@@ -925,44 +952,46 @@
     row = lax.broadcasted_iota(jnp.int32, (samples + 4, samples * devices), 0)
     column = lax.broadcasted_iota(jnp.int32, (samples + 4, samples * devices), 1)
     sums_pick = (column % samples == row).astype(BF16)
-    keep_first, give_first, new_ada, bias_sum = run_whole(
-        first_muon_kernel,
+    new_ada, bias_sum, modes_all, act_all = run_whole(
+        message_kernel,
         place,
-        update_own
-        + update_other
-        + moment_own
-        + moment_other
-        + [m_ada, orders, early_pick, late_pick, sums_pick],
+        message_own + message_other + [m_ada, orders, early_pick, late_pick, sums_pick],
         [
-            struct((rows, hidden), BF16),
-            struct((rows, hidden), BF16),
             struct((rows, half_ada), F32),
             struct((1, bias_here * devices), F32),
+            struct((samples * devices, 6 * features), BF16),
+            struct((samples * devices, features), BF16),
         ],
+        10**9,
+    )
+    returned = run_whole(
+        functools.partial(muon_kernel, rows),
+        place,
+        update_own + update_other + [moment_both, modes_all, act_all],
+        [struct((rows, half_ada), BF16)] * radix,
         10**10,
     )
-    keep_second, give_second = run_whole(
-        second_muon_kernel,
-        place,
-        update_own + update_other + qkv_own + qkv_other,
-        [struct((rows, wide - half_ada), BF16), struct((rows, wide - half_ada), BF16)],
-        3 * 10**9,
-    )
-    taken_first = links.swap_pair(give_first)
-    taken_second = links.swap_pair(give_second)
+    returned = list(returned[:1]) + [
+        links.far(returned[step], stride, step) for step in range(1, radix)
+    ]
     factors = [math.sqrt(max(1.0, aspect)) for aspect in (6.0, 3.0, 1.0, 4.0, 0.25)]
 
-    def finish(keep_first, taken_first, keep_second, taken_second, core, ada, qkv, proj, fc1, fc2):
-        kept = [value.astype(F32) for value in (keep_first, keep_second)]
-        taken = [value.astype(F32) for value in (taken_first, taken_second)]
-        zero = [jnp.where(core == 0, one, other) for one, other in zip(kept, taken)]
-        one = [jnp.where(core == 0, other, one) for one, other in zip(kept, taken)]
+    def finish(role, zero, one, two, three, ada, qkv, proj, fc1, fc2):
+        blocks = [value.astype(F32) for value in (zero, one, two, three)]
+
+        def of_role(chosen, extent):
+            value = blocks[0][:, :extent]
+            for step in range(1, 4):
+                value = jnp.where((role ^ step) == chosen, blocks[step][:, :extent], value)
+            return value
+
+        small = of_role(3, half_qkv + half_proj)
         parts = (
-            zero[0][:, :half_ada],
-            zero[1][:, :half_qkv],
-            one[1][:, :half_proj],
-            one[0][:, :half_fc],
-            one[0][:, half_fc:hidden],
+            of_role(0, half_ada),
+            small[:, :half_qkv],
+            small[:, half_qkv:],
+            of_role(1, half_fc),
+            of_role(2, half_fc),
         )
         return [
             master * (1.0 - matrix_rate * decay_rate) - matrix_rate * factor * part
@@ -971,11 +1000,8 @@
 
     new_weights = fused(
         finish,
-        keep_first,
-        taken_first,
-        keep_second,
-        taken_second,
-        jnp.broadcast_to(core.astype(jnp.int32), (1, 1)),
+        role_array,
+        *returned,
         w_ada,
         w_qkv,
         w_proj,

time: 290 us -> 243 us (0.84)
  waiting for transfers between devices: 76.6 us -> 39 us
  Pallas kernels: 122 us -> 114 us
    ppermute x41 -> x38, waiting for transfers between devices: 74.5 us -> 35.9 us  [swap(): return lax.ppermute(value, AXES, pairs)]
    pallas_call x4, Pallas kernels: 28.7 us -> 22.7 us  [run_whole(): pl.pallas_call(kernel, in_specs=[SMEM_WHOLE] + [vmem] * len(operands), ou...]
    pallas_call x15 -> x13, Pallas kernels: 29.3 us -> 26 us  [fused(): pl.pallas_call(kernel, out_shape=[struct(member.shape, member.dtype) for...]
    unnamed x149 -> x133, local copies, waits for them, and re-layouts: 15.6 us -> 12.9 us
    ppermute x24 -> x18, starting transfers between devices: 6 us -> 3.97 us  [swap_pair(): lax.ppermute(value, AXES, [(i, i ^ 1) for i in range(2 * self.groups)])]
    ppermute x41 -> x38, starting transfers between devices: 55.2 us -> 57 us  [swap(): return lax.ppermute(value, AXES, pairs)]
  transfers between devices with their start and end apart: 65 -> 56, of which waited for: 23 -> 14; matrix products, arithmetic and copies ran while one was open for 3% -> 4% of each run, Pallas kernels for 26% -> 20%
where the time goes in v1:
time: 243 us; the launch traced here: 240 us
  Pallas kernels  114 us (47%)
  starting transfers between devices  60.9 us (25%)
  waiting for transfers between devices  39 us (16%)
  local copies, waits for them, and re-layouts  18.5 us (8%)
  other arithmetic  6.25 us (3%)
    ppermute x38, starting transfers between devices, swap(): return lax.ppermute(value, AXES, pairs)  57 us
    ppermute x38, waiting for transfers between devices, swap(): return lax.ppermute(value, AXES, pairs)  35.9 us
    pallas_call x1, Pallas kernels, run_hidden(): pl.pallas_call(hidden_kernel, grid=(samples,), in_specs=[SMEM_WHOLE, SMEM...  30.1 us
    pallas_call x13, Pallas kernels, fused(): pl.pallas_call(kernel, out_shape=[struct(member.shape, member.dtype) for...  26 us
    pallas_call x4, Pallas kernels, run_whole(): pl.pallas_call(kernel, in_specs=[SMEM_WHOLE] + [vmem] * len(operands), ou...  22.7 us
    pallas_call x3, Pallas kernels, run_scores(): pl.pallas_call(scores_kernel, grid=(count,), in_specs=[each(member.shape,...  16.7 us
    unnamed x133, local copies, waits for them, and re-layouts  12.9 us
    pallas_call x1, Pallas kernels, run_closing(): pl.pallas_call(functools.partial(closing_kernel, starts), grid=(samples,)...  9.46 us
  transfers between devices with their start and end apart: 56, of which 14 were waited for; matrix products, arithmetic and copies ran while one was open for 4% of the time, Pallas kernels for 20%

profile of v1, /device:TPU:0, one launch (start us, length us, event | category | flops | bytes accessed | tf_op | source)
XLA Modules:
  0.0 239.6 jit_solution(5750063175813389606)
XLA Ops:
  2.0 1.6 shard_map.288.refs_0_
  3.7 3.0 %collective-permute-start = (bf16[24,1792]{1,0:T(8,128)(2,1)}, bf16[24,1792]{1,0:T(8,128)(2,1)S(1)}, u32[]{:S(2)}, u32[]{:S(2)}) collective-permute-start(bf16[24,1792]{1,0:T(8,128)(2,1)} %shard_map.288.refs_0_), channel_id=1, source_target_pairs={{0,8},{1,9},{2,10},{3,11},{4,12},{5,13},{6,14},{7,15},{8,0},{9,1},... | collective-permute-start | bytes 258056 | tf_op jit(solution)/shard_map/ppermute | solution.py:104
  6.7 2.6 %collective-permute-start.1 = (bf16[24,1792]{1,0:T(8,128)(2,1)}, bf16[24,1792]{1,0:T(8,128)(2,1)S(1)}, u32[]{:S(2)}, u32[]{:S(2)}) collective-permute-start(bf16[24,1792]{1,0:T(8,128)(2,1)} %shard_map.288.refs_0_), channel_id=1, source_target_pairs={{0,16},{1,17},{2,18},{3,19},{4,20},{5,21},{6,22},{7,23},{8,24},{9,... | collective-permute-start | bytes 258056 | tf_op jit(solution)/shard_map/ppermute | solution.py:104
  9.4 7.0 %collective-permute-done.1.refs_2_ = bf16[24,1792]{1,0:T(8,128)(2,1)S(1)} collective-permute-done((bf16[24,1792]{1,0:T(8,128)(2,1)}, bf16[24,1792]{1,0:T(8,128)(2,1)S(1)}, u32[]{:S(2)}, u32[]{:S(2)}) %collective-permute-start.1) | collective-permute-done | bytes 86048 | tf_op jit(solution)/shard_map/ppermute | solution.py:104
  17.7 1.8 shard_map.289.refs_0_
  21.0 1.6 shard_map.290.refs_0_
  23.5 2.2 collective-permute-start.4
  27.1 1.6 collective-permute-start.13
  28.9 7.3 %collective-permute-done.4.refs_2_ = bf16[24,2944]{1,0:T(8,128)(2,1)S(1)} collective-permute-done((bf16[24,2944]{1,0:T(8,128)(2,1)}, bf16[24,2944]{1,0:T(8,128)(2,1)S(1)}, u32[]{:S(2)}, u32[]{:S(2)}) %collective-permute-start.4) | collective-permute-done | bytes 141344 | tf_op jit(solution)/shard_map/ppermute | solution.py:104
  37.5 1.9 shard_map.291.refs_0_
  39.5 1.5 collective-permute-start.6
  41.6 1.6 collective-permute-start.14
  46.6 5.9 %collective-permute-done.6.refs_1_ = bf16[96,2944]{1,0:T(8,128)(2,1)S(1)} collective-permute-done((bf16[96,2944]{1,0:T(8,128)(2,1)}, bf16[96,2944]{1,0:T(8,128)(2,1)S(1)}, u32[]{:S(2)}, u32[]{:S(2)}) %collective-permute-start.6) | collective-permute-done | bytes 565280 | tf_op jit(solution)/shard_map/ppermute | solution.py:104
  52.5 2.5 %collective-permute-start.8 = (bf16[96,2944]{1,0:T(8,128)(2,1)S(1)}, bf16[96,2944]{1,0:T(8,128)(2,1)S(1)}, u32[]{:S(2)}, u32[]{:S(2)}) collective-permute-start(bf16[96,2944]{1,0:T(8,128)(2,1)S(1)} %collective-permute-done.6.refs_1_), channel_id=1, source_target_pairs={{0,2},{1,5},{2,0},{3,7},{4,6},{5,1},{6,4},{7,3},{8,10},{9,13},{10,... | collective-permute-start | bytes 1695752 | tf_op jit(solution)/shard_map/ppermute | solution.py:104
  61.1 4.4 %shard_map.292 = (bf16[384,1152]{1,0:T(8,128)(2,1)}, f32[1,5376]{1,0:T(1,128)}, f32[4,1,2304]{2,1,0:T(1,128)}, bf16[4,384]{1,0:T(4,128)(2,1)}) custom-call(s32[3]{0:T(128)} %pad_add_fusion.2.place_ref, bf16[96,1792]{1,0:T(8,128)(2,1)} %shard_map.289.refs_0_, bf16[96,1792]{1,0:T(8,128)(2,1)} %copy-done.43, bf16[96,1792]{1,0:T(8,128)(2,1)} %copy-done.44, ...), custom_call_target="tpu_custom_call" | custom-call | flops 2000000000 | bytes 1048576 | tf_op jit(solution)/shard_map/pallas_call | solution.py:639
  65.6 8.6 %shard_map.293 = (bf16[4,256,384]{2,1,0:T(8,128)(2,1)}, bf16[4,256,1152]{2,1,0:T(8,128)(2,1)}, f32[4,256,128]{2,1,0:T(8,128)}, bf16[4,256,384]{2,1,0:T(8,128)(2,1)}) custom-call(bf16[4,256,384]{2,1,0:T(8,128)(2,1)} %bitcast.19, f32[4,1,2304]{2,1,0:T(1,128)} %get-tuple-element.78.modes_ref.refs_11_.refs_5_, f32[1,5376]{1,0:T(1,128)} %get-tuple-element.79.bias_ref.refs_12_, ...), custom_call_target="tpu_custom_call" | custom-call | flops 11796480000 | bytes 1048576 | tf_op jit(solution)/shard_map/pallas_call | solution.py:656
  75.7 30.1 %shard_map.294 = (bf16[4,256,384]{2,1,0:T(8,128)(2,1)}, bf16[4,256,384]{2,1,0:T(8,128)(2,1)}, f32[4,256,384]{2,1,0:T(8,128)}, f32[4,1,2304]{2,1,0:T(1,128)}, f32...) custom-call(s32[3]{0:T(128)} %pad_add_fusion.2.place_ref, ...), custom_call_target="tpu_custom_call" | custom-call | flops 23592960000 | bytes 1048576 | tf_op jit(solution)/shard_map/pallas_call | solution.py:681
  106.2 3.0 %collective-permute-done.20.refs_1_ = bf16[384,1792]{1,0:T(8,128)(2,1)S(1)} collective-permute-done((bf16[384,1792]{1,0:T(8,128)(2,1)}, bf16[384,1792]{1,0:T(8,128)(2,1)S(1)}, u32[]{:S(2)}, u32[]{:S(2)}) %collective-permute-start.20) | collective-permute-done | bytes 1376288 | tf_op jit(solution)/shard_map/ppermute | solution.py:107
  110.3 3.6 %shard_map.296 = (f32[192,1792]{1,0:T(8,128)}, bf16[192,1792]{1,0:T(8,128)(2,1)}) custom-call(f32[384,1792]{1,0:T(8,128)} %get-tuple-element.86.refs_0_, bf16[384,1792]{1,0:T(8,128)(2,1)} %copy-done), custom_call_target="tpu_custom_call" | custom-call | bytes 8257536 | tf_op jit(solution)/shard_map/pallas_call | solution.py:77
  114.6 4.7 %shard_map.295.refs_0_ = bf16[1,256,1152]{2,1,0:T(8,128)(2,1)} custom-call(bf16[4,256,1152]{2,1,0:T(8,128)(2,1)} %get-tuple-element.83.qkv_ref, f32[4,256,128]{2,1,0:T(8,128)} %get-tuple-element.84.lse_ref, bf16[4,256,384]{2,1,0:T(8,128)(2,1)} %get-tuple-element.92.dmix_ref), custom_call_target="tpu_custom_call" | custom-call | flops 2949120000 | bytes 1048576 | tf_op jit(solution)/shard_map/pallas_call | solution.py:705
  119.3 5.8 %collective-permute-done.21.refs_1_ = bf16[192,1792]{1,0:T(8,128)(2,1)S(1)} collective-permute-done((bf16[192,1792]{1,0:T(8,128)(2,1)}, bf16[192,1792]{1,0:T(8,128)(2,1)S(1)}, u32[]{:S(2)}, u32[]{:S(2)}) %collective-permute-start.21) | collective-permute-done | bytes 688160 | tf_op jit(solution)/shard_map/ppermute | solution.py:104
  125.9 2.6 %shard_map.298 = (f32[96,1792]{1,0:T(8,128)}, bf16[96,1792]{1,0:T(8,128)(2,1)}) custom-call(f32[192,1792]{1,0:T(8,128)} %get-tuple-element.88.refs_0_, bf16[192,1792]{1,0:T(8,128)(2,1)} %copy-done.1), custom_call_target="tpu_custom_call" | custom-call | bytes 4128768 | tf_op jit(solution)/shard_map/pallas_call | solution.py:77
  128.5 2.4 %collective-permute-start.22 = (bf16[96,1792]{1,0:T(8,128)(2,1)}, bf16[96,1792]{1,0:T(8,128)(2,1)S(1)}, u32[]{:S(2)}, u32[]{:S(2)}) collective-permute-start(bf16[96,1792]{1,0:T(8,128)(2,1)} %get-tuple-element.94), channel_id=1, source_target_pairs={{0,4},{1,3},{2,6},{3,1},{4,0},{5,7},{6,2},{7,5},{8,12},{9,11},{10,... | collective-permute-start | bytes 1032200 | tf_op jit(solution)/shard_map/ppermute | solution.py:104
  130.9 7.4 %shard_map.297.refs_1_ = bf16[2,256,1152]{2,1,0:T(8,128)(2,1)} custom-call(bf16[4,256,1152]{2,1,0:T(8,128)(2,1)} %get-tuple-element.83.qkv_ref, f32[4,256,128]{2,1,0:T(8,128)} %get-tuple-element.84.lse_ref, bf16[4,256,384]{2,1,0:T(8,128)(2,1)} %get-tuple-element.92.dmix_ref), custom_call_target="tpu_custom_call" | custom-call | flops 5898240000 | bytes 1048576 | tf_op jit(solution)/shard_map/pallas_call | solution.py:705
  138.2 4.7 %shard_map.299.refs_2_ = bf16[1,256,1152]{2,1,0:T(8,128)(2,1)} custom-call(bf16[4,256,1152]{2,1,0:T(8,128)(2,1)} %get-tuple-element.83.qkv_ref, f32[4,256,128]{2,1,0:T(8,128)} %get-tuple-element.84.lse_ref, bf16[4,256,384]{2,1,0:T(8,128)(2,1)} %get-tuple-element.92.dmix_ref), custom_call_target="tpu_custom_call" | custom-call | flops 2949120000 | bytes 1048576 | tf_op jit(solution)/shard_map/pallas_call | solution.py:705
  143.7 2.0 shard_map.300
  145.6 9.5 %shard_map.301 = (f32[4,256,384]{2,1,0:T(8,128)}, bf16[4,1,2304]{2,1,0:T(2,128)(2,1)}, bf16[8,1792]{1,0:T(8,128)(2,1)}, f32[384,640]{1,0:T(8,128)}, bf16[384,640]{1,0:T(8,128)(2,1)}) custom-call(s32[3]{0:T(128)} %pad_add_fusion.2.place_ref, bf16[1,256,1152]{2,1,0:T(8,128)(2,1)} %shard_map.295.refs_0_, bf16[2,256,1152]{2,1,0:T(8,128)(2,1)} %shard_map.297.refs_1_, ...), custom_call_target="tpu_custom_call" | custom-call | flops 7864320000 | bytes 1048576 | tf_op jit(solution)/shard_map/pallas_call | solution.py:733
  155.2 2.9 %collective-permute-start.23 = (bf16[8,1792]{1,0:T(8,128)(2,1)}, bf16[8,1792]{1,0:T(8,128)(2,1)S(1)}, u32[]{:S(2)}, u32[]{:S(2)}) collective-permute-start(bf16[8,1792]{1,0:T(8,128)(2,1)} %get-tuple-element.104.refs_0_), channel_id=1, source_target_pairs={{0,8},{1,9},{2,10},{3,11},{4,12},{5,13},{6,14},{7,15},{8,0},{9,1},... | collective-permute-start | bytes 86024 | tf_op jit(solution)/shard_map/ppermute | solution.py:104
  161.5 2.2 shard_map.305
  164.7 2.5 %collective-permute-start.39 = (bf16[96,640]{1,0:T(8,128)(2,1)}, bf16[96,640]{1,0:T(8,128)(2,1)S(1)}, u32[]{:S(2)}, u32[]{:S(2)}) collective-permute-start(bf16[96,640]{1,0:T(8,128)(2,1)} %get-tuple-element.114), channel_id=1, source_target_pairs={{0,6},{1,7},{2,4},{3,5},{4,2},{5,3},{6,0},{7,1},{8,14},{9,15},{10,... | collective-permute-start | bytes 368648 | tf_op jit(solution)/shard_map/ppermute | solution.py:104
  168.2 2.2 collective-permute-start.34
  171.9 2.3 collective-permute-start.35
  175.0 1.8 shard_map.306
  176.8 2.5 %collective-permute-start.41 = (bf16[24,640]{1,0:T(8,128)(2,1)}, bf16[24,640]{1,0:T(8,128)(2,1)S(1)}, u32[]{:S(2)}, u32[]{:S(2)}) collective-permute-start(bf16[24,640]{1,0:T(8,128)(2,1)} %get-tuple-element.117), channel_id=1, source_target_pairs={{0,16},{1,17},{2,18},{3,19},{4,20},{5,21},{6,22},{7,23},{8,24},{9,... | collective-permute-start | bytes 92168 | tf_op jit(solution)/shard_map/ppermute | solution.py:104
  179.3 1.9 collective-permute-start.42
  181.9 3.3 %collective-permute-done.42.refs_8_ = bf16[24,640]{1,0:T(8,128)(2,1)S(1)} collective-permute-done((bf16[24,640]{1,0:T(8,128)(2,1)}, bf16[24,640]{1,0:T(8,128)(2,1)S(1)}, u32[]{:S(2)}, u32[]{:S(2)}) %collective-permute-start.42) | collective-permute-done | bytes 30752 | tf_op jit(solution)/shard_map/ppermute | solution.py:104
  185.8 2.0 shard_map.307
  187.8 2.5 %collective-permute-start.44 = (bf16[24,768]{1,0:T(8,128)(2,1)}, bf16[24,768]{1,0:T(8,128)(2,1)S(1)}, u32[]{:S(2)}, u32[]{:S(2)}) collective-permute-start(bf16[24,768]{1,0:T(8,128)(2,1)} %get-tuple-element.125), channel_id=1, source_target_pairs={{0,16},{1,17},{2,18},{3,19},{4,20},{5,21},{6,22},{7,23},{8,24},{9,... | collective-permute-start | bytes 110600 | tf_op jit(solution)/shard_map/ppermute | solution.py:104
  190.3 1.9 collective-permute-start.45
  192.7 1.6 collective-permute-start.28
  194.3 1.9 collective-permute-done.45.refs_3_
  198.3 2.1 collective-permute-start.46
  205.7 4.6 %shard_map.302 = f32[4,384]{1,0:T(4,128)} custom-call(s32[3]{0:T(128)} %pad_add_fusion.2.place_ref, bf16[96,1792]{1,0:T(8,128)(2,1)} %shard_map.289.refs_0_, bf16[96,1792]{1,0:T(8,128)(2,1)} %copy-done.43, bf16[96,1792]{1,0:T(8,128)(2,1)} %copy-done.44, bf16[96,1792]{1,0:T(8,128)(2,1)} %collective-permute-done.15.refs_3_, ...), custom_call_target="tpu_custom_call" | custom-call | flops 1000000000 | bytes 1048576 | tf_op jit(solution)/shard_map/pallas_call | solution.py:639
  213.5 2.9 %shard_map.304 = (f32[24,1152]{1,0:T(8,128)}, f32[1,5376]{1,0:T(1,128)}, bf16[128,2304]{1,0:T(8,128)(2,1)}, bf16[128,384]{1,0:T(8,128)(2,1)}) custom-call(s32[3]{0:T(128)} %pad_add_fusion.2.place_ref, bf16[32,1792]{1,0:T(8,128)(2,1)} %shard_map.303.refs_0_, bf16[32,1792]{1,0:T(8,128)(2,1)} %copy-done.55, bf16[32,1792]{1,0:T(8,128)(2,1)} %copy-done.56, ...), custom_call_target="tpu_custom_call" | custom-call | flops 1000000000 | bytes 1048576 | tf_op jit(solution)/shard_map/pallas_call | solution.py:639
  218.1 10.8 %shard_map.309 = (bf16[24,1152]{1,0:T(8,128)(2,1)}, bf16[24,1152]{1,0:T(8,128)(2,1)}, bf16[24,1152]{1,0:T(8,128)(2,1)}, bf16[24,1152]{1,0:T(8,128)(2,1)}) custom-call(s32[3]{0:T(128)} %pad_add_fusion.2.place_ref, bf16[96,768]{1,0:T(8,128)(2,1)} %shard_map.308.refs_0_, bf16[96,768]{1,0:T(8,128)(2,1)} %copy-done.48, bf16[96,768]{1,0:T(8,128)(2,1)} %copy-done.49, ...), custom_call_target="tpu_custom_call" | custom-call | flops 10000000000 | bytes 1048576 | tf_op jit(solution)/shard_map/pallas_call | solution.py:639
  229.8 3.4 %collective-permute-start.55 = (bf16[24,1152]{1,0:T(8,128)(2,1)}, bf16[24,1152]{1,0:T(8,128)(2,1)S(1)}, u32[]{:S(2)}, u32[]{:S(2)}) collective-permute-start(bf16[24,1152]{1,0:T(8,128)(2,1)} %get-tuple-element.133), channel_id=1, source_target_pairs={{0,24},{1,25},{2,26},{3,27},{4,28},{5,29},{6,30},{7,31},{8,16},{9,... | collective-permute-start | bytes 165896 | tf_op jit(solution)/shard_map/ppermute | solution.py:104
  234.0 2.9 %collective-permute-done.54.refs_3_ = bf16[24,1152]{1,0:T(8,128)(2,1)S(1)} collective-permute-done((bf16[24,1152]{1,0:T(8,128)(2,1)}, bf16[24,1152]{1,0:T(8,128)(2,1)S(1)}, u32[]{:S(2)}, u32[]{:S(2)}) %collective-permute-start.54) | collective-permute-done | bytes 55328 | tf_op jit(solution)/shard_map/ppermute | solution.py:104
  237.5 2.0 shard_map.310
  (242 shorter events, 47.5 us)
Async XLA Ops:
  3.7 5.8 %collective-permute-start = (bf16[24,1792]{1,0:T(8,128)(2,1)}, bf16[24,1792]{1,0:T(8,128)(2,1)S(1)}, u32[]{:S(2)}, u32[]{:S(2)}) collective-permute-start(bf16[24,1792]{1,0:T(8,128)(2,1)} %shard_map.288.refs_0_), channel_id=1, source_target_pairs={{0,8},{1,9},{2,10},{3,11},{4,12},{5,13},{6,14},{7,15},{8,0},{9,1},... | collective-permute-start | bytes 258056 | tf_op jit(solution)/shard_map/ppermute | solution.py:104
  6.7 9.7 %collective-permute-start.1 = (bf16[24,1792]{1,0:T(8,128)(2,1)}, bf16[24,1792]{1,0:T(8,128)(2,1)S(1)}, u32[]{:S(2)}, u32[]{:S(2)}) collective-permute-start(bf16[24,1792]{1,0:T(8,128)(2,1)} %shard_map.288.refs_0_), channel_id=1, source_target_pairs={{0,16},{1,17},{2,18},{3,19},{4,20},{5,21},{6,22},{7,23},{8,24},{9,... | collective-permute-start | bytes 258056 | tf_op jit(solution)/shard_map/ppermute | solution.py:104
  9.3 7.1 %collective-permute-start.2 = (bf16[24,1792]{1,0:T(8,128)(2,1)}, bf16[24,1792]{1,0:T(8,128)(2,1)S(1)}, u32[]{:S(2)}, u32[]{:S(2)}) collective-permute-start(bf16[24,1792]{1,0:T(8,128)(2,1)} %shard_map.288.refs_0_), channel_id=1, source_target_pairs={{0,24},{1,25},{2,26},{3,27},{4,28},{5,29},{6,30},{7,31},{8,16},{9,... | collective-permute-start | bytes 258056 | tf_op jit(solution)/shard_map/ppermute | solution.py:104
  22.6 6.3 %collective-permute-start.3 = (bf16[24,2944]{1,0:T(8,128)(2,1)}, bf16[24,2944]{1,0:T(8,128)(2,1)S(1)}, u32[]{:S(2)}, u32[]{:S(2)}) collective-permute-start(bf16[24,2944]{1,0:T(8,128)(2,1)} %shard_map.290.refs_0_), channel_id=1, source_target_pairs={{0,8},{1,9},{2,10},{3,11},{4,12},{5,13},{6,14},{7,15},{8,0},{9,1},... | collective-permute-start | bytes 423944 | tf_op jit(solution)/shard_map/ppermute | solution.py:104
  23.5 12.8 %collective-permute-start.4 = (bf16[24,2944]{1,0:T(8,128)(2,1)}, bf16[24,2944]{1,0:T(8,128)(2,1)S(1)}, u32[]{:S(2)}, u32[]{:S(2)}) collective-permute-start(bf16[24,2944]{1,0:T(8,128)(2,1)} %shard_map.290.refs_0_), channel_id=1, source_target_pairs={{0,16},{1,17},{2,18},{3,19},{4,20},{5,21},{6,22},{7,23},{8,24},{9,... | collective-permute-start | bytes 423944 | tf_op jit(solution)/shard_map/ppermute | solution.py:104
  25.6 10.6 %collective-permute-start.5 = (bf16[24,2944]{1,0:T(8,128)(2,1)}, bf16[24,2944]{1,0:T(8,128)(2,1)S(1)}, u32[]{:S(2)}, u32[]{:S(2)}) collective-permute-start(bf16[24,2944]{1,0:T(8,128)(2,1)} %shard_map.290.refs_0_), channel_id=1, source_target_pairs={{0,24},{1,25},{2,26},{3,27},{4,28},{5,29},{6,30},{7,31},{8,16},{9,... | collective-permute-start | bytes 423944 | tf_op jit(solution)/shard_map/ppermute | solution.py:104
  27.1 16.0 %collective-permute-start.13 = (bf16[96,1792]{1,0:T(8,128)(2,1)}, bf16[96,1792]{1,0:T(8,128)(2,1)S(1)}, u32[]{:S(2)}, u32[]{:S(2)}) collective-permute-start(bf16[96,1792]{1,0:T(8,128)(2,1)} %shard_map.289.refs_0_), channel_id=1, source_target_pairs={{0,4},{1,3},{2,6},{3,1},{4,0},{5,7},{6,2},{7,5},{8,12},{9,11},{10,... | collective-permute-start | bytes 1032200 | tf_op jit(solution)/shard_map/ppermute | solution.py:104
  39.5 13.0 %collective-permute-start.6 = (bf16[96,2944]{1,0:T(8,128)(2,1)}, bf16[96,2944]{1,0:T(8,128)(2,1)S(1)}, u32[]{:S(2)}, u32[]{:S(2)}) collective-permute-start(bf16[96,2944]{1,0:T(8,128)(2,1)} %shard_map.291.refs_0_), channel_id=1, source_target_pairs={{0,4},{1,3},{2,6},{3,1},{4,0},{5,7},{6,2},{7,5},{8,12},{9,11},{10,... | collective-permute-start | bytes 1695752 | tf_op jit(solution)/shard_map/ppermute | solution.py:104
  41.6 15.3 %collective-permute-start.14 = (bf16[96,1792]{1,0:T(8,128)(2,1)S(1)}, bf16[96,1792]{1,0:T(8,128)(2,1)S(1)}, u32[]{:S(2)}, u32[]{:S(2)}) collective-permute-start(bf16[96,1792]{1,0:T(8,128)(2,1)S(1)} %copy-done.4), channel_id=1, source_target_pairs={{0,2},{1,5},{2,0},{3,7},{4,6},{5,1},{6,4},{7,3},{8,10},{9,13},{10,... | collective-permute-start | bytes 1032200 | tf_op jit(solution)/shard_map/ppermute | solution.py:104
  43.1 13.7 %collective-permute-start.16 = (bf16[96,1792]{1,0:T(8,128)(2,1)S(1)}, bf16[96,1792]{1,0:T(8,128)(2,1)}, u32[]{:S(2)}, u32[]{:S(2)}) collective-permute-start(bf16[96,1792]{1,0:T(8,128)(2,1)S(1)} %copy-done.4), channel_id=1, source_target_pairs={{0,1},{1,0},{2,3},{3,2},{4,5},{5,4},{6,7},{7,6},{8,9},{9,8},{10,11... | collective-permute-start | bytes 1032200 | tf_op jit(solution)/shard_map/ppermute | solution.py:107
  43.1 14.2 %collective-permute-start.15 = (bf16[96,1792]{1,0:T(8,128)(2,1)S(1)}, bf16[96,1792]{1,0:T(8,128)(2,1)}, u32[]{:S(2)}, u32[]{:S(2)}) collective-permute-start(bf16[96,1792]{1,0:T(8,128)(2,1)S(1)} %collective-permute-done.13.refs_1_), channel_id=1, source_target_pairs={{0,2},{1,5},{2,0},{3,7},{4,6},{5,1},{6,4},{7,3},{8,10},{9,13},{10,... | collective-permute-start | bytes 1032200 | tf_op jit(solution)/shard_map/ppermute | solution.py:104
  44.5 15.2 %collective-permute-start.7 = (bf16[96,2944]{1,0:T(8,128)(2,1)}, bf16[96,2944]{1,0:T(8,128)(2,1)S(1)}, u32[]{:S(2)}, u32[]{:S(2)}) collective-permute-start(bf16[96,2944]{1,0:T(8,128)(2,1)} %shard_map.291.refs_0_), channel_id=1, source_target_pairs={{0,2},{1,5},{2,0},{3,7},{4,6},{5,1},{6,4},{7,3},{8,10},{9,13},{10,... | collective-permute-start | bytes 1695752 | tf_op jit(solution)/shard_map/ppermute | solution.py:104
  52.5 13.0 %collective-permute-start.8 = (bf16[96,2944]{1,0:T(8,128)(2,1)S(1)}, bf16[96,2944]{1,0:T(8,128)(2,1)S(1)}, u32[]{:S(2)}, u32[]{:S(2)}) collective-permute-start(bf16[96,2944]{1,0:T(8,128)(2,1)S(1)} %collective-permute-done.6.refs_1_), channel_id=1, source_target_pairs={{0,2},{1,5},{2,0},{3,7},{4,6},{5,1},{6,4},{7,3},{8,10},{9,13},{10,... | collective-permute-start | bytes 1695752 | tf_op jit(solution)/shard_map/ppermute | solution.py:104
  59.1 15.2 %collective-permute-start.9 = (bf16[96,2944]{1,0:T(8,128)(2,1)S(1)}, bf16[96,2944]{1,0:T(8,128)(2,1)S(1)}, u32[]{:S(2)}, u32[]{:S(2)}) collective-permute-start(bf16[96,2944]{1,0:T(8,128)(2,1)S(1)} %copy-done.2), channel_id=1, source_target_pairs={{0,1},{1,0},{2,3},{3,2},{4,5},{5,4},{6,7},{7,6},{8,9},{9,8},{10,11... | collective-permute-start | bytes 1695752 | tf_op jit(solution)/shard_map/ppermute | solution.py:107
  59.6 14.7 %collective-permute-start.10 = (bf16[96,2944]{1,0:T(8,128)(2,1)S(1)}, bf16[96,2944]{1,0:T(8,128)(2,1)S(1)}, u32[]{:S(2)}, u32[]{:S(2)}) collective-permute-start(bf16[96,2944]{1,0:T(8,128)(2,1)S(1)} %collective-permute-done.6.refs_1_), channel_id=1, source_target_pairs={{0,1},{1,0},{2,3},{3,2},{4,5},{5,4},{6,7},{7,6},{8,9},{9,8},{10,11... | collective-permute-start | bytes 1695752 | tf_op jit(solution)/shard_map/ppermute | solution.py:107
  59.7 14.6 %collective-permute-start.11 = (bf16[96,2944]{1,0:T(8,128)(2,1)S(1)}, bf16[96,2944]{1,0:T(8,128)(2,1)S(1)}, u32[]{:S(2)}, u32[]{:S(2)}) collective-permute-start(bf16[96,2944]{1,0:T(8,128)(2,1)S(1)} %collective-permute-done.7.refs_2_), channel_id=1, source_target_pairs={{0,1},{1,0},{2,3},{3,2},{4,5},{5,4},{6,7},{7,6},{8,9},{9,8},{10,11... | collective-permute-start | bytes 1695752 | tf_op jit(solution)/shard_map/ppermute | solution.py:107
  65.5 8.9 %collective-permute-start.12 = (bf16[96,2944]{1,0:T(8,128)(2,1)S(1)}, bf16[96,2944]{1,0:T(8,128)(2,1)S(1)}, u32[]{:S(2)}, u32[]{:S(2)}) collective-permute-start(bf16[96,2944]{1,0:T(8,128)(2,1)S(1)} %collective-permute-done.8.refs_3_), channel_id=1, source_target_pairs={{0,1},{1,0},{2,3},{3,2},{4,5},{5,4},{6,7},{7,6},{8,9},{9,8},{10,11... | collective-permute-start | bytes 1695752 | tf_op jit(solution)/shard_map/ppermute | solution.py:107
  113.9 11.1 %collective-permute-start.21 = (bf16[192,1792]{1,0:T(8,128)(2,1)}, bf16[192,1792]{1,0:T(8,128)(2,1)S(1)}, u32[]{:S(2)}, u32[]{:S(2)}) collective-permute-start(bf16[192,1792]{1,0:T(8,128)(2,1)} %get-tuple-element.90), channel_id=1, source_target_pairs={{0,2},{1,5},{2,0},{3,7},{4,6},{5,1},{6,4},{7,3},{8,10},{9,13},{10,... | collective-permute-start | bytes 2064392 | tf_op jit(solution)/shard_map/ppermute | solution.py:104
  128.5 14.5 %collective-permute-start.22 = (bf16[96,1792]{1,0:T(8,128)(2,1)}, bf16[96,1792]{1,0:T(8,128)(2,1)S(1)}, u32[]{:S(2)}, u32[]{:S(2)}) collective-permute-start(bf16[96,1792]{1,0:T(8,128)(2,1)} %get-tuple-element.94), channel_id=1, source_target_pairs={{0,4},{1,3},{2,6},{3,1},{4,0},{5,7},{6,2},{7,5},{8,12},{9,11},{10,... | collective-permute-start | bytes 1032200 | tf_op jit(solution)/shard_map/ppermute | solution.py:104
  155.1 5.6 %collective-permute-start.36 = (bf16[384,640]{1,0:T(8,128)(2,1)}, bf16[384,640]{1,0:T(8,128)(2,1)S(1)}, u32[]{:S(2)}, u32[]{:S(2)}) collective-permute-start(bf16[384,640]{1,0:T(8,128)(2,1)} %get-tuple-element.110), channel_id=1, source_target_pairs={{0,1},{1,0},{2,3},{3,2},{4,5},{5,4},{6,7},{7,6},{8,9},{9,8},{10,11... | collective-permute-start | bytes 1474568 | tf_op jit(solution)/shard_map/ppermute | solution.py:107
  155.2 9.5 %collective-permute-start.23 = (bf16[8,1792]{1,0:T(8,128)(2,1)}, bf16[8,1792]{1,0:T(8,128)(2,1)S(1)}, u32[]{:S(2)}, u32[]{:S(2)}) collective-permute-start(bf16[8,1792]{1,0:T(8,128)(2,1)} %get-tuple-element.104.refs_0_), channel_id=1, source_target_pairs={{0,8},{1,9},{2,10},{3,11},{4,12},{5,13},{6,14},{7,15},{8,0},{9,1},... | collective-permute-start | bytes 86024 | tf_op jit(solution)/shard_map/ppermute | solution.py:104
  158.1 9.0 %collective-permute-start.24 = (bf16[8,1792]{1,0:T(8,128)(2,1)}, bf16[8,1792]{1,0:T(8,128)(2,1)S(1)}, u32[]{:S(2)}, u32[]{:S(2)}) collective-permute-start(bf16[8,1792]{1,0:T(8,128)(2,1)} %get-tuple-element.104.refs_0_), channel_id=1, source_target_pairs={{0,16},{1,17},{2,18},{3,19},{4,20},{5,21},{6,22},{7,23},{8,24},{9,... | collective-permute-start | bytes 86024 | tf_op jit(solution)/shard_map/ppermute | solution.py:104
  159.3 8.8 %collective-permute-start.25 = (bf16[8,1792]{1,0:T(8,128)(2,1)}, bf16[8,1792]{1,0:T(8,128)(2,1)S(1)}, u32[]{:S(2)}, u32[]{:S(2)}) collective-permute-start(bf16[8,1792]{1,0:T(8,128)(2,1)} %get-tuple-element.104.refs_0_), channel_id=1, source_target_pairs={{0,24},{1,25},{2,26},{3,27},{4,28},{5,29},{6,30},{7,31},{8,16},{9,... | collective-permute-start | bytes 86024 | tf_op jit(solution)/shard_map/ppermute | solution.py:104
  163.7 8.2 %collective-permute-start.37 = (bf16[96,640]{1,0:T(8,128)(2,1)}, bf16[96,640]{1,0:T(8,128)(2,1)S(1)}, u32[]{:S(2)}, u32[]{:S(2)}) collective-permute-start(bf16[96,640]{1,0:T(8,128)(2,1)} %get-tuple-element.112), channel_id=1, source_target_pairs={{0,4},{1,3},{2,6},{3,1},{4,0},{5,7},{6,2},{7,5},{8,12},{9,11},{10,... | collective-permute-start | bytes 368648 | tf_op jit(solution)/shard_map/ppermute | solution.py:104
  164.2 10.1 %collective-permute-start.38 = (bf16[96,640]{1,0:T(8,128)(2,1)}, bf16[96,640]{1,0:T(8,128)(2,1)S(1)}, u32[]{:S(2)}, u32[]{:S(2)}) collective-permute-start(bf16[96,640]{1,0:T(8,128)(2,1)} %get-tuple-element.113), channel_id=1, source_target_pairs={{0,2},{1,5},{2,0},{3,7},{4,6},{5,1},{6,4},{7,3},{8,10},{9,13},{10,... | collective-permute-start | bytes 368648 | tf_op jit(solution)/shard_map/ppermute | solution.py:104
  164.7 9.6 %collective-permute-start.39 = (bf16[96,640]{1,0:T(8,128)(2,1)}, bf16[96,640]{1,0:T(8,128)(2,1)S(1)}, u32[]{:S(2)}, u32[]{:S(2)}) collective-permute-start(bf16[96,640]{1,0:T(8,128)(2,1)} %get-tuple-element.114), channel_id=1, source_target_pairs={{0,6},{1,7},{2,4},{3,5},{4,2},{5,3},{6,0},{7,1},{8,14},{9,15},{10,... | collective-permute-start | bytes 368648 | tf_op jit(solution)/shard_map/ppermute | solution.py:104
  167.2 9.6 %collective-permute-start.33 = (bf16[24,1792]{1,0:T(8,128)(2,1)S(1)}, bf16[24,1792]{1,0:T(8,128)(2,1)S(1)}, u32[]{:S(2)}, u32[]{:S(2)}) collective-permute-start(bf16[24,1792]{1,0:T(8,128)(2,1)S(1)} %copy-done.64), channel_id=1, source_target_pairs={{0,8},{1,9},{2,10},{3,11},{4,12},{5,13},{6,14},{7,15},{8,0},{9,1},... | collective-permute-start | bytes 258056 | tf_op jit(solution)/shard_map/ppermute | solution.py:104
  168.2 11.1 %collective-permute-start.34 = (bf16[24,1792]{1,0:T(8,128)(2,1)S(1)}, bf16[24,1792]{1,0:T(8,128)(2,1)S(1)}, u32[]{:S(2)}, u32[]{:S(2)}) collective-permute-start(bf16[24,1792]{1,0:T(8,128)(2,1)S(1)} %copy-done.63), channel_id=1, source_target_pairs={{0,16},{1,17},{2,18},{3,19},{4,20},{5,21},{6,22},{7,23},{8,24},{9,... | collective-permute-start | bytes 258056 | tf_op jit(solution)/shard_map/ppermute | solution.py:104
  171.9 9.3 %collective-permute-start.35 = (bf16[24,1792]{1,0:T(8,128)(2,1)S(1)}, bf16[24,1792]{1,0:T(8,128)(2,1)S(1)}, u32[]{:S(2)}, u32[]{:S(2)}) collective-permute-start(bf16[24,1792]{1,0:T(8,128)(2,1)S(1)} %copy-done.62), channel_id=1, source_target_pairs={{0,24},{1,25},{2,26},{3,27},{4,28},{5,29},{6,30},{7,31},{8,16},{9,... | collective-permute-start | bytes 258056 | tf_op jit(solution)/shard_map/ppermute | solution.py:104
  174.3 18.4 %collective-permute-start.26 = (bf16[32,1792]{1,0:T(8,128)(2,1)}, bf16[32,1792]{1,0:T(8,128)(2,1)S(1)}, u32[]{:S(2)}, u32[]{:S(2)}) collective-permute-start(bf16[32,1792]{1,0:T(8,128)(2,1)} %shard_map.303.refs_0_), channel_id=1, source_target_pairs={{0,4},{1,3},{2,6},{3,1},{4,0},{5,7},{6,2},{7,5},{8,12},{9,11},{10,... | collective-permute-start | bytes 344072 | tf_op jit(solution)/shard_map/ppermute | solution.py:104
  176.8 5.1 %collective-permute-start.41 = (bf16[24,640]{1,0:T(8,128)(2,1)}, bf16[24,640]{1,0:T(8,128)(2,1)S(1)}, u32[]{:S(2)}, u32[]{:S(2)}) collective-permute-start(bf16[24,640]{1,0:T(8,128)(2,1)} %get-tuple-element.117), channel_id=1, source_target_pairs={{0,16},{1,17},{2,18},{3,19},{4,20},{5,21},{6,22},{7,23},{8,24},{9,... | collective-permute-start | bytes 92168 | tf_op jit(solution)/shard_map/ppermute | solution.py:104
  179.3 5.9 %collective-permute-start.42 = (bf16[24,640]{1,0:T(8,128)(2,1)}, bf16[24,640]{1,0:T(8,128)(2,1)S(1)}, u32[]{:S(2)}, u32[]{:S(2)}) collective-permute-start(bf16[24,640]{1,0:T(8,128)(2,1)} %get-tuple-element.118), channel_id=1, source_target_pairs={{0,24},{1,25},{2,26},{3,27},{4,28},{5,29},{6,30},{7,31},{8,16},{9,... | collective-permute-start | bytes 92168 | tf_op jit(solution)/shard_map/ppermute | solution.py:104
  187.8 6.5 %collective-permute-start.44 = (bf16[24,768]{1,0:T(8,128)(2,1)}, bf16[24,768]{1,0:T(8,128)(2,1)S(1)}, u32[]{:S(2)}, u32[]{:S(2)}) collective-permute-start(bf16[24,768]{1,0:T(8,128)(2,1)} %get-tuple-element.125), channel_id=1, source_target_pairs={{0,16},{1,17},{2,18},{3,19},{4,20},{5,21},{6,22},{7,23},{8,24},{9,... | collective-permute-start | bytes 110600 | tf_op jit(solution)/shard_map/ppermute | solution.py:104
  190.3 6.0 %collective-permute-start.45 = (bf16[24,768]{1,0:T(8,128)(2,1)}, bf16[24,768]{1,0:T(8,128)(2,1)S(1)}, u32[]{:S(2)}, u32[]{:S(2)}) collective-permute-start(bf16[24,768]{1,0:T(8,128)(2,1)} %get-tuple-element.126), channel_id=1, source_target_pairs={{0,24},{1,25},{2,26},{3,27},{4,28},{5,29},{6,30},{7,31},{8,16},{9,... | collective-permute-start | bytes 110600 | tf_op jit(solution)/shard_map/ppermute | solution.py:104
  192.2 9.1 %collective-permute-start.27 = (bf16[32,1792]{1,0:T(8,128)(2,1)}, bf16[32,1792]{1,0:T(8,128)(2,1)S(1)}, u32[]{:S(2)}, u32[]{:S(2)}) collective-permute-start(bf16[32,1792]{1,0:T(8,128)(2,1)} %shard_map.303.refs_0_), channel_id=1, source_target_pairs={{0,2},{1,5},{2,0},{3,7},{4,6},{5,1},{6,4},{7,3},{8,10},{9,13},{10,... | collective-permute-start | bytes 344072 | tf_op jit(solution)/shard_map/ppermute | solution.py:104
  192.7 9.2 %collective-permute-start.29 = (bf16[32,1792]{1,0:T(8,128)(2,1)}, bf16[32,1792]{1,0:T(8,128)(2,1)S(1)}, u32[]{:S(2)}, u32[]{:S(2)}) collective-permute-start(bf16[32,1792]{1,0:T(8,128)(2,1)} %shard_map.303.refs_0_), channel_id=1, source_target_pairs={{0,1},{1,0},{2,3},{3,2},{4,5},{5,4},{6,7},{7,6},{8,9},{9,8},{10,11... | collective-permute-start | bytes 344072 | tf_op jit(solution)/shard_map/ppermute | solution.py:107
  192.7 9.0 %collective-permute-start.28 = (bf16[32,1792]{1,0:T(8,128)(2,1)S(1)}, bf16[32,1792]{1,0:T(8,128)(2,1)S(1)}, u32[]{:S(2)}, u32[]{:S(2)}) collective-permute-start(bf16[32,1792]{1,0:T(8,128)(2,1)S(1)} %collective-permute-done.26.refs_1_), channel_id=1, source_target_pairs={{0,2},{1,5},{2,0},{3,7},{4,6},{5,1},{6,4},{7,3},{8,10},{9,13},{10,... | collective-permute-start | bytes 344072 | tf_op jit(solution)/shard_map/ppermute | solution.py:104
  198.3 5.5 %collective-permute-start.46 = (bf16[96,768]{1,0:T(8,128)(2,1)}, bf16[96,768]{1,0:T(8,128)(2,1)S(1)}, u32[]{:S(2)}, u32[]{:S(2)}) collective-permute-start(bf16[96,768]{1,0:T(8,128)(2,1)} %shard_map.308.refs_0_), channel_id=1, source_target_pairs={{0,4},{1,3},{2,6},{3,1},{4,0},{5,7},{6,2},{7,5},{8,12},{9,11},{10,... | collective-permute-start | bytes 442376 | tf_op jit(solution)/shard_map/ppermute | solution.py:104
  201.2 10.4 %collective-permute-start.30 = (bf16[32,1792]{1,0:T(8,128)(2,1)S(1)}, bf16[32,1792]{1,0:T(8,128)(2,1)S(1)}, u32[]{:S(2)}, u32[]{:S(2)}) collective-permute-start(bf16[32,1792]{1,0:T(8,128)(2,1)S(1)} %collective-permute-done.26.refs_1_), channel_id=1, source_target_pairs={{0,1},{1,0},{2,3},{3,2},{4,5},{5,4},{6,7},{7,6},{8,9},{9,8},{10,11... | collective-permute-start | bytes 344072 | tf_op jit(solution)/shard_map/ppermute | solution.py:107
  201.3 10.5 %collective-permute-start.31 = (bf16[32,1792]{1,0:T(8,128)(2,1)S(1)}, bf16[32,1792]{1,0:T(8,128)(2,1)S(1)}, u32[]{:S(2)}, u32[]{:S(2)}) collective-permute-start(bf16[32,1792]{1,0:T(8,128)(2,1)S(1)} %collective-permute-done.27.refs_2_), channel_id=1, source_target_pairs={{0,1},{1,0},{2,3},{3,2},{4,5},{5,4},{6,7},{7,6},{8,9},{9,8},{10,11... | collective-permute-start | bytes 344072 | tf_op jit(solution)/shard_map/ppermute | solution.py:107
  201.8 11.1 %collective-permute-start.32 = (bf16[32,1792]{1,0:T(8,128)(2,1)S(1)}, bf16[32,1792]{1,0:T(8,128)(2,1)S(1)}, u32[]{:S(2)}, u32[]{:S(2)}) collective-permute-start(bf16[32,1792]{1,0:T(8,128)(2,1)S(1)} %collective-permute-done.28.refs_3_), channel_id=1, source_target_pairs={{0,1},{1,0},{2,3},{3,2},{4,5},{5,4},{6,7},{7,6},{8,9},{9,8},{10,11... | collective-permute-start | bytes 344072 | tf_op jit(solution)/shard_map/ppermute | solution.py:107
  201.9 10.5 %collective-permute-start.47 = (bf16[96,768]{1,0:T(8,128)(2,1)}, bf16[96,768]{1,0:T(8,128)(2,1)S(1)}, u32[]{:S(2)}, u32[]{:S(2)}) collective-permute-start(bf16[96,768]{1,0:T(8,128)(2,1)} %shard_map.308.refs_0_), channel_id=1, source_target_pairs={{0,2},{1,5},{2,0},{3,7},{4,6},{5,1},{6,4},{7,3},{8,10},{9,13},{10,... | collective-permute-start | bytes 442376 | tf_op jit(solution)/shard_map/ppermute | solution.py:104
  203.8 8.7 %collective-permute-start.48 = (bf16[96,768]{1,0:T(8,128)(2,1)S(1)}, bf16[96,768]{1,0:T(8,128)(2,1)S(1)}, u32[]{:S(2)}, u32[]{:S(2)}) collective-permute-start(bf16[96,768]{1,0:T(8,128)(2,1)S(1)} %collective-permute-done.46.refs_1_), channel_id=1, source_target_pairs={{0,2},{1,5},{2,0},{3,7},{4,6},{5,1},{6,4},{7,3},{8,10},{9,13},{10,... | collective-permute-start | bytes 442376 | tf_op jit(solution)/shard_map/ppermute | solution.py:104
  211.7 5.5 %collective-permute-start.49 = (bf16[96,768]{1,0:T(8,128)(2,1)S(1)}, bf16[96,768]{1,0:T(8,128)(2,1)S(1)}, u32[]{:S(2)}, u32[]{:S(2)}) collective-permute-start(bf16[96,768]{1,0:T(8,128)(2,1)S(1)} %copy-done.6), channel_id=1, source_target_pairs={{0,1},{1,0},{2,3},{3,2},{4,5},{5,4},{6,7},{7,6},{8,9},{9,8},{10,11... | collective-permute-start | bytes 442376 | tf_op jit(solution)/shard_map/ppermute | solution.py:107
  211.8 5.4 %collective-permute-start.50 = (bf16[96,768]{1,0:T(8,128)(2,1)S(1)}, bf16[96,768]{1,0:T(8,128)(2,1)S(1)}, u32[]{:S(2)}, u32[]{:S(2)}) collective-permute-start(bf16[96,768]{1,0:T(8,128)(2,1)S(1)} %collective-permute-done.46.refs_1_), channel_id=1, source_target_pairs={{0,1},{1,0},{2,3},{3,2},{4,5},{5,4},{6,7},{7,6},{8,9},{9,8},{10,11... | collective-permute-start | bytes 442376 | tf_op jit(solution)/shard_map/ppermute | solution.py:107
  228.8 5.1 %collective-permute-start.53 = (bf16[24,1152]{1,0:T(8,128)(2,1)}, bf16[24,1152]{1,0:T(8,128)(2,1)S(1)}, u32[]{:S(2)}, u32[]{:S(2)}) collective-permute-start(bf16[24,1152]{1,0:T(8,128)(2,1)} %get-tuple-element.131), channel_id=1, source_target_pairs={{0,8},{1,9},{2,10},{3,11},{4,12},{5,13},{6,14},{7,15},{8,0},{9,1},... | collective-permute-start | bytes 165896 | tf_op jit(solution)/shard_map/ppermute | solution.py:104
  228.8 8.0 %collective-permute-start.54 = (bf16[24,1152]{1,0:T(8,128)(2,1)}, bf16[24,1152]{1,0:T(8,128)(2,1)S(1)}, u32[]{:S(2)}, u32[]{:S(2)}) collective-permute-start(bf16[24,1152]{1,0:T(8,128)(2,1)} %get-tuple-element.132), channel_id=1, source_target_pairs={{0,16},{1,17},{2,18},{3,19},{4,20},{5,21},{6,22},{7,23},{8,24},{9,... | collective-permute-start | bytes 165896 | tf_op jit(solution)/shard_map/ppermute | solution.py:104
  229.8 7.1 %collective-permute-start.55 = (bf16[24,1152]{1,0:T(8,128)(2,1)}, bf16[24,1152]{1,0:T(8,128)(2,1)S(1)}, u32[]{:S(2)}, u32[]{:S(2)}) collective-permute-start(bf16[24,1152]{1,0:T(8,128)(2,1)} %get-tuple-element.133), channel_id=1, source_target_pairs={{0,24},{1,25},{2,26},{3,27},{4,28},{5,29},{6,30},{7,31},{8,16},{9,... | collective-permute-start | bytes 165896 | tf_op jit(solution)/shard_map/ppermute | solution.py:104
  (74 other events, 467.8 us)
